TPU v7x, 256 devices: a whole 4x4x8 slice. The times are simulated.
256 devices in a mesh: dp: 4 (over x), seq: 16 (over z, core), mp: 4 (over y).
Axes of the slice: x: 4, y: 4, z: 8, core: 2. Of those that a mesh axis runs over, the one named last changes fastest.
Arguments:
- patches: bfloat16 [16384, 3072], P(('dp', 'seq'), 'mp'), may hold values from -20 to 20
- image_of: int32 [16384], P(('dp', 'seq')), may hold values from 0 to 31, as said below
- prompt_of: int32 [4, 32], P('dp', 'seq'), may hold values from 0 to 15
- text_len: int32 [4, 16], P('dp'), may hold values from 1 to 256, as said below
- text_kv: bfloat16 [64, 256, 2, 1536], P('dp', 'seq', None, 'mp'), may hold values from -70 to 70
- w_qkv: bfloat16 [3072, 3, 1536], P(None, None, 'mp'), may hold values from -0.109375 to 0.109375
- w_out: bfloat16 [1536, 3072], P('mp'), may hold values from -0.15625 to 0.15625
- pre_gain: float32 [3072], replicated, may hold values from 0.1 to 1.9
- pre_bias: float32 [3072], replicated, may hold values from -3 to 3
- post_gain: float32 [3072], replicated, may hold values from 0.1 to 1.9
- post_bias: float32 [3072], replicated, may hold values from -3 to 3
Outputs:
- block_out: bfloat16 [16384, 3072], P(('dp', 'seq'), 'mp')
Inputs may be any that keep to these rules, and one draw needn't show every extreme that they name: `image_of`: the rows of one device name each image at most 16 times; in every data-parallel group one image is named exactly 16 times by the rows of every device of that group. `text_len`: in every data-parallel group some prompt has all 256 tokens live.
All inputs are finite; a program needn't handle non-finite values.
Results may differ from a plain program's by a relative error of at most 0.011.
Values may be sent and summed in bfloat16 or wider, within the bound.
A program may use at most 128 MiB of HBM per device.

v0:
```python
import math

import jax
import jax.numpy as jnp
from jax import lax
from jax.sharding import PartitionSpec as P

HD = 128


epsilon = 1e-05


def layer_norm(values_in, gain_vec, bias_vec):
    average = jnp.mean(values_in, axis=-1, keepdims=True)
    centered = values_in - average
    spread = jnp.mean(centered * centered, axis=-1, keepdims=True)
    return centered * lax.rsqrt(spread + epsilon) * gain_vec + bias_vec


def slot_layout(image_of, local_images, seq_count):
    tok_rows = image_of.shape[0]
    images_all = local_images * seq_count
    slot_depth = 2 * tok_rows // images_all
    slot_span = seq_count * slot_depth
    onehot = (image_of[:, None] == jnp.arange(images_all, dtype=jnp.int32)[None, :]).astype(
        jnp.int32
    )
    ranking = jnp.sum(jnp.cumsum(onehot, axis=0) * onehot, axis=1) - 1
    owner_index = image_of // local_images
    within = image_of % local_images
    position = within * slot_span + owner_index * slot_depth + ranking
    total_slots = local_images * slot_span
    source_row = (
        jnp.zeros((total_slots,), jnp.int32).at[position].set(jnp.arange(tok_rows, dtype=jnp.int32))
    )
    filled = (
        jnp.zeros((total_slots,), jnp.bfloat16)
        .at[position]
        .set(jnp.ones((tok_rows,), jnp.bfloat16))
    )
    return (position, source_row, filled, slot_span)


def dispatch(row_data, layout, local_images):
    position, source_row, filled, slot_span = layout
    buffer = jnp.take(row_data, source_row, axis=0) * filled[:, None]
    buffer = buffer.reshape(local_images, slot_span, row_data.shape[1])
    return (
        lax.all_to_all(buffer, "seq", split_axis=1, concat_axis=1, tiled=True),
        lax.all_to_all(
            filled.reshape(local_images, slot_span), "seq", split_axis=1, concat_axis=1, tiled=True
        ),
    )


def collect(slot_data, layout):
    position = layout[0]
    returned = lax.all_to_all(slot_data, "seq", split_axis=1, concat_axis=1, tiled=True)
    return jnp.take(returned.reshape(-1, slot_data.shape[2]), position, axis=0)


def project(row_data, w_qkv, pre_gain, pre_bias):
    gathered = lax.all_gather(row_data, "mp", axis=1, tiled=True)
    normed = layer_norm(gathered.astype(jnp.float32), pre_gain, pre_bias).astype(jnp.bfloat16)
    merged = w_qkv.reshape(w_qkv.shape[0], -1)
    return jnp.dot(normed, merged, preferred_element_type=jnp.float32).astype(jnp.bfloat16)


def attend(projected, filled, prompts, chosen, lengths):
    image_count, slot_span, triple = projected.shape
    head_cols = triple // 3
    head_count = head_cols // HD
    softmax_scale = 1.0 / math.sqrt(HD)
    queries = projected[:, :, :head_cols].reshape(image_count, slot_span, head_count, HD)
    image_key_rows = projected[:, :, head_cols : 2 * head_cols].reshape(
        image_count, slot_span, head_count, HD
    )
    vals_img = projected[:, :, 2 * head_cols :].reshape(image_count, slot_span, head_count, HD)
    txt_len = chosen.shape[1]
    keys_txt = chosen[:, :, 0].reshape(image_count, txt_len, head_count, HD)
    vals_txt = chosen[:, :, 1].reshape(image_count, txt_len, head_count, HD)
    prompt_count = lengths.shape[0]
    prompt_match = prompts[:, None] == jnp.arange(prompt_count, dtype=jnp.int32)[None, :]
    image_len = jnp.sum(jnp.where(prompt_match, lengths[None, :], 0), axis=1)
    token_live = jnp.arange(txt_len, dtype=jnp.int32)[None, :] < image_len[:, None]
    image_score_matrix = (
        jnp.einsum("ilhd,imhd->ihlm", queries, image_key_rows, preferred_element_type=jnp.float32)
        * softmax_scale
    )
    image_score_matrix = jnp.where((filled > 0)[:, None, None, :], image_score_matrix, -jnp.inf)
    scores_txt = (
        jnp.einsum("ilhd,ithd->ihlt", queries, keys_txt, preferred_element_type=jnp.float32)
        * softmax_scale
    )
    scores_txt = jnp.where(token_live[:, None, None, :], scores_txt, -jnp.inf)
    scores = jnp.concatenate([image_score_matrix, scores_txt], axis=-1)
    highest = jnp.max(scores, axis=-1, keepdims=True)
    exponent = jnp.exp(scores - highest)
    attention_probs = (exponent / jnp.sum(exponent, axis=-1, keepdims=True)).astype(jnp.bfloat16)
    joint_value_rows = jnp.concatenate([vals_img, vals_txt], axis=1)
    mixed_output = jnp.einsum(
        "ihlm,imhd->ilhd", attention_probs, joint_value_rows, preferred_element_type=jnp.float32
    )
    return mixed_output.astype(jnp.bfloat16).reshape(image_count, slot_span, head_cols)


def finish(attended, residual, w_out, post_gain, post_bias):
    partial_sum = jnp.dot(attended, w_out, preferred_element_type=jnp.float32)
    share_cols = residual.shape[1]
    full_cols = partial_sum.shape[1]
    offset = lax.axis_index("mp") * share_cols
    gain_part = lax.dynamic_slice_in_dim(post_gain, offset, share_cols)
    bias_part = lax.dynamic_slice_in_dim(post_bias, offset, share_cols)
    owned_part = lax.psum_scatter(partial_sum, "mp", scatter_dimension=1, tiled=True)
    totals = lax.psum((jnp.sum(owned_part, axis=1), jnp.sum(owned_part * owned_part, axis=1)), "mp")
    average = (totals[0] / full_cols)[:, None]
    spread = (totals[1] / full_cols)[:, None] - average * average
    normed = (owned_part - average) * lax.rsqrt(spread + epsilon) * gain_part + bias_part
    return (residual.astype(jnp.float32) + normed).astype(jnp.bfloat16)


def shards(
    patches,
    image_of,
    prompt_of,
    text_len,
    text_kv,
    w_qkv,
    w_out,
    pre_gain,
    pre_bias,
    post_gain,
    post_bias,
):
    seq_count = lax.axis_size("seq")
    local_images = prompt_of.shape[1]
    layout = slot_layout(image_of, local_images, seq_count)
    slot_span = layout[3]
    prompts = prompt_of[0]
    lengths = text_len[0]
    text_all = lax.all_gather(text_kv, "seq", axis=1, tiled=True)
    chosen = jnp.take(text_all, prompts, axis=0)
    arrived, filled = dispatch(patches, layout, local_images)
    slot_rows = arrived.reshape(local_images * slot_span, arrived.shape[2])
    projected = project(slot_rows, w_qkv, pre_gain, pre_bias)
    attended = attend(
        projected.reshape(local_images, slot_span, -1), filled, prompts, chosen, lengths
    )
    finished = finish(
        attended.reshape(local_images * slot_span, -1), slot_rows, w_out, post_gain, post_bias
    )
    result = collect(finished.reshape(local_images, slot_span, -1), layout)
    return result


def solution(mesh):
    placed = (
        P(("dp", "seq"), "mp"),
        P(("dp", "seq")),
        P("dp", "seq"),
        P("dp", None),
        P("dp", "seq", None, "mp"),
        P(None, None, "mp"),
        P("mp", None),
        P(),
        P(),
        P(),
        P(),
    )
    return jax.shard_map(
        shards, mesh=mesh, in_specs=placed, out_specs=P(("dp", "seq"), "mp"), check_vma=False
    )
```

profile of v0, /device:TPU:2, one launch (start us, length us, event | category | flops | bytes accessed | tf_op | source)
XLA Modules:
  0.0 269.9 jit_solution(16353884575686637461)
XLA Ops:
  6.5 0.8 fusion.26
  7.4 0.6 reduce-window.6
  7.9 0.2 slice_reduce_fusion
  8.2 0.8 fusion.25
  9.0 1.2 compare_and_fusion.2
  10.2 1.4 scatter_custom_fusion
  11.6 2.2 scatter_custom_fusion.1
  13.8 0.1 copy.83
  14.0 0.2 copy.81
  14.2 3.4 %gather_fusion = bf16[512,768]{1,0:T(8,128)(2,1)S(1)} fusion(bf16[256,768]{1,0:T(8,128)(2,1)} %param.11, s32[1024]{0:T(1024)S(1)} %pad_clamp_fusion.2), kind=kCustom, calls=%fused_computation | custom fusion | bytes 1574912 | tf_op jit(solution)/shard_map/jit(_take)/gather | solution.py:47
  17.6 1.6 fusion.20
  19.3 0.0 copy-start.12
  19.3 0.0 copy-start.13
  19.3 30.9 %all_to_all.19 = bf16[2,256,768]{2,0,1:T(2,128)(2,1)S(1)} all-to-all(bf16[2,256,768]{2,0,1:T(2,128)(2,1)S(1)} %fusion.20), channel_id=1, replica_groups=mesh['dp'=4,'seq'=16,'mp'=4] {'seq'}, dimensions={1} | all-to-all | bytes 1572864 | tf_op jit(solution)/shard_map/all_to_all | solution.py:50
  50.2 1.0 copy.84
  51.2 0.0 all-gather.3.cloned.1.call-update
  51.2 0.0 all-gather.5.cloned.1.call-start
  51.3 0.8 copy.87
  52.1 0.0 all-gather.5.cloned.1.call-update
  52.1 0.1 all_to_all.13
  52.2 0.6 copy.89
  52.8 3.5 %all-to-all-start.1 = ((bf16[2,16,16]{2,0,1:T(2,128)(2,1)}), bf16[2,16,16]{2,0,1:T(2,128)(2,1)S(1)}, u32[]{:S(2)}, u32[]{:S(2)}) async-start(bf16[2,16,16]{2,0,1:T(2,128)(2,1)} %copy.89), calls=%async_computation.1 | async-start | bytes 16384 | tf_op jit(solution)/shard_map/all_to_all | solution.py:51
  56.3 0.2 reduce-scatter.2.cloned.1.call-start
  56.5 0.2 fusion.30
  56.7 0.6 compare_and_fusion
  57.3 0.7 iota_compare_fusion.2
  58.0 10.3 %copy.85 = bf16[3072,3,384]{0,2,1:T(8,128)(2,1)} copy(bf16[3072,3,384]{2,0,1:T(8,128)(2,1)} %param.16) | data formatting | bytes 14155776 | tf_op args[5]
  68.3 0.1 gt.15
  68.4 22.9 %all-gather.3.cloned.1.call-done = bf16[512,3072]{1,0:T(8,128)(2,1)} async-done(((bf16[512,768]{1,0:T(8,128)(2,1)}), bf16[512,3072]{1,0:T(8,128)(2,1)}) %all-gather.3.cloned.1.call-update) | async-done | bytes 3145744 | tf_op jit(solution)/shard_map/all_gather | solution.py:64
  91.3 2.5 convert_reduce_fusion
  93.8 0.0 copy-start.11
  93.9 0.3 copy-done.1
  94.1 1.0 fusion.2
  95.1 7.7 %fusion.13 = bf16[512,1152]{1,0:T(8,128)(2,1)S(1)} fusion(bf16[3072,1152]{0,1:T(8,128)(2,1)} %bitcast.50, bf16[512,3072]{1,0:T(8,128)(2,1)S(1)} %copy-done.1, f32[3072]{0:T(1024)S(1)} %copy-done.10, f32[3072]{0:T(1024)S(1)} %copy-done.11, f32[512]{0:T(512)S(1)} %add_rsqrt_fusion.1, f32[512]{0:T(512)S(1)} %broadcast_multiply_fusion.1), kind=kOutput, calls=%fused_computation.21 | convolution fusion | flops 3633905664 | bytes 11431936 | tf_op jit(solution)/shard_map/dot_general | solution.py:67
  102.8 0.9 fusion.39
  103.7 1.2 copy.107
  104.9 0.9 copy.108
  105.8 1.0 copy.86
  106.7 2.6 fusion.41
  109.3 30.1 %all-gather.5.cloned.1.call-done = bf16[16,256,2,384]{3,1,2,0:T(8,128)(2,1)} async-done(((bf16[16,16,2,384]{3,1,2,0:T(8,128)(2,1)}), bf16[16,256,2,384]{3,1,2,0:T(8,128)(2,1)}) %all-gather.5.cloned.1.call-update) | async-done | bytes 6291472 | tf_op jit(solution)/shard_map/all_gather | solution.py:142
  139.4 3.5 %gather_fusion.1 = bf16[2,256,2,384]{3,1,2,0:T(8,128)(2,1)S(1)} fusion(bf16[16,256,2,384]{3,1,2,0:T(8,128)(2,1)} %all-gather.5.cloned.1.call-done, s32[1024]{0:T(1024)S(1)} %pad_clamp_fusion.1), kind=kCustom, calls=%fused_computation.1 | custom fusion | bytes 1572872 | tf_op jit(solution)/shard_map/jit(_take)/gather | solution.py:143
  142.9 0.8 broadcast_select_fusion.1
  143.8 0.1 fusion.40
  143.8 0.9 copy.95
  144.8 0.2 copy.88
  145.0 1.6 fusion.42
  146.6 0.4 fusion.16
  147.0 0.7 fusion.19
  147.8 0.4 copy.99
  148.2 0.1 copy.110
  148.3 4.5 %fusion.43 = f32[512,3072]{1,0:T(8,128)} fusion(bf16[512,384]{0,1:T(8,128)(2,1)S(1)} %bitcast.56, bf16[384,3072]{1,0:T(8,128)(2,1)S(1)} %copy-done), kind=kOutput, calls=%fused_computation.83 | convolution fusion | flops 1207959552 | bytes 9043968 | tf_op jit(solution)/shard_map/dot_general | solution.py:109
  152.8 0.0 reduce-scatter.2.cloned.1.call-update
  152.8 0.8 dynamic_slice.6
  153.6 0.8 dynamic_slice.7
  154.4 63.7 %reduce-scatter.2.cloned.1.call-done = f32[512,768]{1,0:T(8,128)} async-done(((f32[512,3072]{1,0:T(8,128)}), f32[512,768]{1,0:T(8,128)}) %reduce-scatter.2.cloned.1.call-update) | async-done | bytes 1572880 | tf_op jit(solution)/shard_map/reduce_scatter | solution.py:115
  218.1 1.7 fusion.38
  219.8 8.8 %all-reduce = (f32[512]{0:T(512)S(1)}, f32[512]{0:T(512)S(1)}) all-reduce(f32[512]{0:T(512)S(1)} %get-tuple-element.6, f32[512]{0:T(512)S(1)} %get-tuple-element.5), channel_id=1, replica_groups=mesh['dp'=4,'seq'=16,'mp'=4] {'mp'}, use_global_device_ids=true, to_apply=%region_15.16 | all-reduce | flops 1024 | bytes 8192 | tf_op jit(solution)/shard_map/psum | solution.py:116
  228.6 1.8 add_convert_fusion
  230.4 1.7 copy.100
  232.1 7.2 %all-to-all-start.2 = ((bf16[2,256,768]{2,0,1:T(2,128)(2,1)}), bf16[2,256,768]{2,0,1:T(2,128)(2,1)}, u32[]{:S(2)}, u32[]{:S(2)}) async-start(bf16[2,256,768]{2,0,1:T(2,128)(2,1)} %copy.100), calls=%async_computation.3 | async-start | bytes 1572864 | tf_op jit(solution)/shard_map/all_to_all | solution.py:59
  239.3 20.7 %all-to-all-done.2 = bf16[2,256,768]{2,0,1:T(2,128)(2,1)} async-done(((bf16[2,256,768]{2,0,1:T(2,128)(2,1)}), bf16[2,256,768]{2,0,1:T(2,128)(2,1)}, u32[]{:S(2)}, u32[]{:S(2)}) %all-to-all-start.2) | async-done | bytes 786464 | tf_op jit(solution)/shard_map/all_to_all | solution.py:59
  260.1 1.2 copy.101
  261.3 1.2 gather_fusion.2
  262.5 0.9 broadcast_select_fusion.2
  (44 shorter events, 0.2 us)
Async XLA Ops:
  6.5 141.7 %copy-start = (bf16[384,3072]{1,0:T(8,128)(2,1)S(1)}, bf16[384,3072]{1,0:T(8,128)(2,1)}, u32[]{:S(2)}) copy-start(bf16[384,3072]{1,0:T(8,128)(2,1)} %param.17) | copy-start | bytes 7077892
  6.5 84.8 %all-gather.3.cloned.1.call-start = ((), (), s32[]{:S(2)}) async-start(), calls=%async_computation.4 | async-start | bytes 3932160 | tf_op jit(solution)/shard_map/all_gather | solution.py:64
  10.2 3.8 %copy-start.6 = (s32[256]{0:T(256)}, s32[256]{0:T(256)S(1)}, u32[]{:S(2)}) copy-start(s32[256]{0:T(256)S(1)} %get-tuple-element.10) | copy-start | bytes 3076
  19.3 32.0 %copy-start.4 = (bf16[16,16,2,384]{3,2,1,0:T(2,128)(2,1)S(1)}, bf16[16,16,2,384]{3,2,1,0:T(2,128)(2,1)}, u32[]{:S(2)}) copy-start(bf16[16,16,2,384]{3,2,1,0:T(2,128)(2,1)} %param.15) | copy-start | bytes 1179652
  19.3 37.2 %copy-start.12 = (s32[1,16]{1,0:T(1,128)S(1)}, s32[1,16]{1,0:T(1,128)}, u32[]{:S(2)}) copy-start(s32[1,16]{1,0:T(1,128)} %param.14) | copy-start | bytes 196
  19.3 37.2 %copy-start.13 = (s32[1,2]{1,0:T(1,128)S(1)}, s32[1,2]{1,0:T(1,128)}, u32[]{:S(2)}) copy-start(s32[1,2]{1,0:T(1,128)} %param.13) | copy-start | bytes 28
  51.2 88.2 %all-gather.5.cloned.1.call-start = ((), (), s32[]{:S(2)}) async-start(), calls=%async_computation.5 | async-start | bytes 6684672 | tf_op jit(solution)/shard_map/all_gather | solution.py:142
  52.8 15.5 %all-to-all-start.1 = ((bf16[2,16,16]{2,0,1:T(2,128)(2,1)}), bf16[2,16,16]{2,0,1:T(2,128)(2,1)S(1)}, u32[]{:S(2)}, u32[]{:S(2)}) async-start(bf16[2,16,16]{2,0,1:T(2,128)(2,1)} %copy.89), calls=%async_computation.1 | async-start | bytes 16384 | tf_op jit(solution)/shard_map/all_to_all | solution.py:51
  56.3 161.8 %reduce-scatter.2.cloned.1.call-start = ((), (), s32[]{:S(2)}) async-start(), calls=%async_computation.6 | async-start | bytes 7864320 | tf_op jit(solution)/shard_map/reduce_scatter | solution.py:115
  91.3 2.8 %copy-start.1 = (bf16[512,3072]{1,0:T(8,128)(2,1)S(1)}, bf16[512,3072]{1,0:T(8,128)(2,1)}, u32[]{:S(2)}) copy-start(bf16[512,3072]{1,0:T(8,128)(2,1)} %all-gather.3.cloned.1.call-done) | copy-start | bytes 9437188
  93.8 1.3 copy-start.10
  93.8 1.3 copy-start.11
  142.9 2.1 copy-start.9
  145.0 1.6 copy-start.3
  145.0 2.0 copy-start.5
  152.7 75.8 %copy-start.2 = (bf16[2,256,768]{2,1,0:T(8,128)(2,1)S(1)}, bf16[2,256,768]{2,1,0:T(8,128)(2,1)}, u32[]{:S(2)}) copy-start(bf16[2,256,768]{2,1,0:T(8,128)(2,1)} %copy.84) | copy-start | bytes 2359300
  230.4 8.9 %copy-start.7 = (s32[256]{0:T(256)S(1)}, s32[256]{0:T(256)}, u32[]{:S(2)}) copy-start(s32[256]{0:T(256)} %copy-done.6) | copy-start | bytes 3076
  232.1 27.9 %all-to-all-start.2 = ((bf16[2,256,768]{2,0,1:T(2,128)(2,1)}), bf16[2,256,768]{2,0,1:T(2,128)(2,1)}, u32[]{:S(2)}, u32[]{:S(2)}) async-start(bf16[2,256,768]{2,0,1:T(2,128)(2,1)} %copy.100), calls=%async_computation.3 | async-start | bytes 1572864 | tf_op jit(solution)/shard_map/all_to_all | solution.py:59
  239.3 23.1 %copy-start.8 = (pred[256]{0:T(512)(128)(4,1)S(1)}, pred[256]{0:T(512)(128)(4,1)}, u32[]{:S(2)}) copy-start(pred[256]{0:T(512)(128)(4,1)} %get-tuple-element.9) | copy-start | bytes 772
Sparse Core Ops, SparseCore 0:
  51.3 39.9 all-gather.2
  93.1 46.2 all-gather.4
  152.9 65.1 reduce-scatter.1
where the time goes:
time: 274 us; the launch traced here: 270 us
  waiting for transfers between devices  137 us (50%)
  blocking collectives  39.7 us (14%)
  local copies, waits for them, and re-layouts  35.6 us (13%)
  matrix products  17.1 us (6%)
  other arithmetic  15.7 us (6%)
  between operations  13.5 us (5%)
  starting transfers between devices  10.9 us (4%)
    reduce_scatter x1, waiting for transfers between devices, finish(): lax.psum_scatter(partial_sum, 'mp', scatter_dimension=1, tiled=True)  63.7 us
    all_to_all x1, blocking collectives, dispatch(): lax.all_to_all(buffer, 'seq', split_axis=1, concat_axis=1, tiled=True)  30.9 us
    all_gather x1, waiting for transfers between devices, shards(): text_all = lax.all_gather(text_kv, 'seq', axis=1, tiled=True)  30.1 us
    all_gather x1, waiting for transfers between devices, project(): gathered = lax.all_gather(row_data, 'mp', axis=1, tiled=True)  22.9 us
    all_to_all x1, waiting for transfers between devices, collect(): lax.all_to_all(slot_data, 'seq', split_axis=1, concat_axis=1, tiled=True)  20.7 us
    unnamed x33, local copies, waits for them, and re-layouts  13.6 us
    psum x1, blocking collectives, finish(): lax.psum((jnp.sum(owned_part, axis=1), jnp.sum(owned_part * owned_part, a...  8.79 us
    dot_general x1, matrix products, project(): jnp.dot(normed, merged, preferred_element_type=jnp.float32)  7.7 us
  transfers between devices with their start and end apart: 5, of which 4 were waited for; matrix products, arithmetic and copies ran while one was open for 12% of the time, Pallas kernels for 0%

commit v1 on v0

v1 whole, which is shorter than its diff:
```python
import math

import jax
import jax.numpy as jnp
from jax import lax
from jax.experimental import pallas as pl
from jax.experimental.pallas import tpu as pltpu
from jax.sharding import PartitionSpec as P

HD = 128
EPS = 1e-05
MESH = pl.DeviceIdType.MESH
NEG = -1e30

f32 = jnp.float32
bf16 = jnp.bfloat16
i32 = jnp.int32


def iota(shape, dim):
    return lax.broadcasted_iota(i32, shape, dim)


def fused(
    x_ref, img_ref, prm_ref, len_ref, text_ref, w_ref, wo_ref, pg_ref, pb_ref, qg_ref, qb_ref,
    o_ref,
    xs, xg, xn, wv, wc, qkv, ts, tr, ret, ag, ms, mr, mrs, st, sr, kb,
    zss, zrs, tss, trs, mss, mrsem, yss, yrs, rss, rrs, y2s, y2r, wss, wrs, bss, brs, sss, srs, lsem,
):
    s = lax.axis_index("seq")
    m = lax.axis_index("mp")
    NS, MP = xg.shape[1], xg.shape[0]
    rows = x_ref.shape[0]
    cols = x_ref.shape[1]
    slots = xs.shape[2] * xs.shape[1] * NS
    depth = xs.shape[2]
    nimg = 2 * NS
    heads = qkv.shape[3] // HD
    right = lax.rem(m + 1, MP)
    left = lax.rem(m + MP - 1, MP)
    far = lax.rem(m + 2, MP)
    core = lax.rem(s, 2)
    sib = s + 1 - 2 * core

    def seq_at(k):
        return lax.rem(s + k, NS)

    def step_k(t):
        half = (t + 1) // 2
        return jnp.where(lax.rem(t, 2) == 1, half, lax.rem(NS - half, NS))

    bar = pltpu.get_barrier_semaphore()

    @pl.loop(1, NS)
    def _(k):
        pl.semaphore_signal(bar, inc=1, device_id={"seq": seq_at(k)}, device_id_type=MESH)

    for d in (right, left, far):
        pl.semaphore_signal(bar, inc=1, device_id={"mp": d}, device_id_type=MESH)

    wcp = pltpu.make_async_copy(w_ref, wv, lsem.at[0])
    wcp.start()
    ocp = pltpu.make_async_copy(wo_ref.at[:, pl.ds(pl.multiple_of(m * cols, 128), cols)], wc.at[m], lsem.at[1])
    ocp.start()

    img = img_ref[...]
    onehot = (jnp.broadcast_to(img, (nimg, rows)) == iota((nimg, rows), 0)).astype(f32)
    upto = (iota((rows, rows), 0) <= iota((rows, rows), 1)).astype(bf16)
    cum = jnp.dot(onehot.astype(bf16), upto, preferred_element_type=f32)
    rank = jnp.sum(cum * onehot, axis=0, keepdims=True) - 1.0
    pos = img.astype(f32) * depth + rank
    counts = jnp.sum(onehot, axis=1, keepdims=True)
    crow = jnp.sum(
        jnp.where(iota((nimg, 128), 0) == iota((nimg, 128), 1), jnp.broadcast_to(counts, (nimg, 128)), 0.0),
        axis=0, keepdims=True,
    ).astype(i32)
    lane = iota((1, 128), 1)
    crow = jnp.where(lane == nimg, prm_ref[0, 0], jnp.where(lane == nimg + 1, prm_ref[0, 1], crow))
    ms[...] = crow
    mr[s] = crow
    place = (jnp.broadcast_to(pos, (slots, rows)) == iota((slots, rows), 0).astype(f32)).astype(bf16)
    spread = jnp.dot(place, x_ref[...], preferred_element_type=f32).astype(bf16)
    xs[...] = spread.reshape(xs.shape)
    xg[m, s] = xs[s]

    pl.semaphore_wait(bar, NS - 1 + 3)

    def zcopy(d, c):
        return pltpu.make_async_remote_copy(
            src_ref=xs.at[d], dst_ref=xg.at[m, c], send_sem=zss.at[d], recv_sem=zrs.at[c],
            device_id={"seq": d}, device_id_type=MESH)

    def tcopy(d, c):
        return pltpu.make_async_remote_copy(
            src_ref=ts.at[d], dst_ref=tr.at[c], send_sem=tss.at[d], recv_sem=trs.at[c],
            device_id={"seq": d}, device_id_type=MESH)

    def mcopy(d, c):
        return pltpu.make_async_remote_copy(
            src_ref=ms, dst_ref=mr.at[c], send_sem=mss.at[d], recv_sem=mrsem.at[c],
            device_id={"seq": d}, device_id_type=MESH)

    def rcopy(d, c):
        return pltpu.make_async_remote_copy(
            src_ref=ret.at[d], dst_ref=ag.at[m, c], send_sem=rss.at[d], recv_sem=rrs.at[c],
            device_id={"seq": d}, device_id_type=MESH)

    def relay(buf, ssem, rsem):
        def one(y, c, part, lane_of, to):
            ref = buf.at[y, c] if part is None else buf.at[y, c, part]
            return pltpu.make_async_remote_copy(
                src_ref=ref, dst_ref=ref, send_sem=ssem.at[lane_of, c], recv_sem=rsem.at[lane_of, c],
                device_id={"mp": to}, device_id_type=MESH)

        first = lambda c: (one(m, c, None, 0, right), one(m, c, None, 1, left))
        second = lambda c: (one(left, c, 0, 2, right), one(right, c, 1, 3, left))
        got_left = lambda c: one(left, c, None, 0, right)
        got_right = lambda c: one(right, c, None, 1, left)
        got_far0 = lambda c: one(far, c, 0, 2, right)
        got_far1 = lambda c: one(far, c, 1, 3, left)

        def open_(c):
            a, b = first(c)
            a.start()
            b.start()

        def pass_on(c):
            a, b = second(c)
            got_left(c).wait_recv()
            a.start()
            got_right(c).wait_recv()
            b.start()

        def arrived(c):
            got_far0(c).wait_recv()
            got_far1(c).wait_recv()

        def drain(c):
            for cp in first(c) + second(c):
                cp.wait_send()

        return open_, pass_on, arrived, drain

    @pl.loop(1, NS)
    def _(k):
        mcopy(seq_at(k), s).start()

    @pl.loop(1, NS)
    def _(t):
        zcopy(seq_at(step_k(t)), s).start()

    @pl.loop(1, NS)
    def _(k):
        c = seq_at(k)
        mcopy(c, c).wait()

    scp = pltpu.make_async_copy(mr, mrs, lsem.at[2])
    scp.start()
    scp.wait()

    @pl.loop(0, NS)
    def _(d):
        for i in range(2):
            ts[d, i] = text_ref[mrs[d, 0, nimg + i]]

    tr[s] = ts[s]

    open1, pass1, arrived1, drain1 = relay(xg, yss, yrs)
    LAG1, LAG2 = 2, 4

    def norm_chunk(c):
        parts = [xg[y, c].astype(f32) for y in range(MP)]
        total = sum(jnp.sum(p, axis=-1, keepdims=True) for p in parts)
        mean = total / (MP * cols)
        parts = [p - mean for p in parts]
        var = sum(jnp.sum(p * p, axis=-1, keepdims=True) for p in parts) / (MP * cols)
        inv = lax.rsqrt(var + EPS)
        for y in range(MP):
            g = pg_ref[:, y * cols:(y + 1) * cols].reshape(1, 1, cols)
            b = pb_ref[:, y * cols:(y + 1) * cols].reshape(1, 1, cols)
            n = (parts[y] * inv * g + b).astype(bf16)
            for i in range(2):
                xn[i, c, :, y * cols:(y + 1) * cols] = n[i]

    @pl.loop(0, NS + LAG2)
    def _(t):
        @pl.when(t < NS)
        def _():
            k = step_k(t)
            c = lax.rem(s + NS - k, NS)
            d = seq_at(k)

            @pl.when(t > 0)
            def _():
                zcopy(c, c).wait_recv()

            open1(c)

            @pl.when(t > 0)
            def _():
                zcopy(d, s).wait_send()
                tcopy(d, s).start()

        @pl.when((t >= LAG1) & (t < NS + LAG1))
        def _():
            pass1(lax.rem(s + NS - step_k(t - LAG1), NS))

        @pl.when(t >= LAG2)
        def _():
            c = lax.rem(s + NS - step_k(t - LAG2), NS)
            arrived1(c)
            norm_chunk(c)

    hrows = wc.shape[1] // 2
    mine = pl.ds(pl.multiple_of(core * hrows, 16), hrows)

    def wcopy(y, k):
        return pltpu.make_async_remote_copy(
            src_ref=wo_ref.at[mine, pl.ds(pl.multiple_of(y * cols, 128), cols)], dst_ref=wc.at[m, mine],
            send_sem=wss.at[k], recv_sem=wrs.at[k], device_id={"mp": y}, device_id_type=MESH)

    def wgot(y, k):
        return pltpu.make_async_remote_copy(
            src_ref=wo_ref.at[mine, pl.ds(pl.multiple_of(y * cols, 128), cols)], dst_ref=wc.at[y, mine],
            send_sem=wss.at[k], recv_sem=wrs.at[k], device_id={"mp": y}, device_id_type=MESH)

    other = pl.ds(pl.multiple_of((1 - core) * hrows, 16), hrows)

    def bcopy(y, k, part):
        return pltpu.make_async_remote_copy(
            src_ref=wc.at[y, part], dst_ref=wc.at[y, part], send_sem=bss.at[k], recv_sem=brs.at[k],
            device_id={"seq": sib}, device_id_type=MESH)

    for k in (1, 3, 2):
        wcopy(lax.rem(m + k, MP), k).start()

    wcp.wait()
    normed = xn[...].reshape(slots, MP * cols)

    @pl.loop(0, 3)
    def _(j):
        r = jnp.dot(normed, wv[j], preferred_element_type=f32).astype(bf16)
        qkv[j] = r.reshape(qkv.shape[1:])

    span = NS * depth
    lanes = iota((1, span), 1)
    tlen = NS * depth
    for i in range(2):
        cnt = jnp.zeros((1, span), i32)
        for c in range(NS):
            cnt = jnp.where(lanes // depth == c, mrs[c, 0, 2 * s + i], cnt)
        kb[2 * i] = jnp.where(lax.rem(lanes, depth) < cnt, 0.0, NEG)
        n = len_ref[0, mrs[s, 0, nimg + i]]
        kb[2 * i + 1] = jnp.where(lanes < n, 0.0, NEG)

    @pl.loop(1, NS)
    def _(k):
        c = seq_at(k)
        tcopy(c, c).wait_recv()

    scale = 1.0 / math.sqrt(HD)
    nt = (((1,), (1,)), ((), ()))

    @pl.loop(0, 2)
    def _(i):
        bi = kb[2 * i]
        bt = kb[2 * i + 1]
        for h in range(heads):
            hs = slice(h * HD, (h + 1) * HD)
            q = qkv[0, i, :, hs]
            ki = qkv[1, i, :, hs]
            vi = qkv[2, i, :, hs]
            kt = tr[:, i, 0, :, hs].reshape(tlen, HD)
            vt = tr[:, i, 1, :, hs].reshape(tlen, HD)
            s1 = lax.dot_general(q, ki, nt, preferred_element_type=f32) * scale + bi
            s2 = lax.dot_general(q, kt, nt, preferred_element_type=f32) * scale + bt
            top = jnp.maximum(jnp.max(s1, axis=-1, keepdims=True), jnp.max(s2, axis=-1, keepdims=True))
            e1 = jnp.exp(s1 - top)
            e2 = jnp.exp(s2 - top)
            tot = jnp.sum(e1, axis=-1, keepdims=True) + jnp.sum(e2, axis=-1, keepdims=True)
            inv = 1.0 / tot
            p1 = (e1 * inv).astype(bf16)
            p2 = (e2 * inv).astype(bf16)
            o = jnp.dot(p1, vi, preferred_element_type=f32) + jnp.dot(p2, vt, preferred_element_type=f32)
            ret[:, i, :, hs] = o.astype(bf16).reshape(NS, depth, HD)

    @pl.loop(1, NS)
    def _(t):
        rcopy(seq_at(step_k(t)), s).start()

    ag[m, s] = ret[s]
    for k in (1, 3, 2):
        y = lax.rem(m + MP - k, MP)
        wgot(y, k).wait_recv()
        bcopy(y, k, mine).start()

    open2, pass2, arrived2, drain2 = relay(ag, y2s, y2r)

    @pl.loop(0, NS + LAG1)
    def _(t):
        @pl.when(t < NS)
        def _():
            k = step_k(t)
            c = lax.rem(s + NS - k, NS)

            @pl.when(t > 0)
            def _():
                rcopy(c, c).wait_recv()

            open2(c)

        @pl.when(t >= LAG1)
        def _():
            pass2(lax.rem(s + NS - step_k(t - LAG1), NS))

    @pl.loop(0, NS)
    def _(c):
        arrived2(c)

    ocp.wait()
    for k in (1, 3, 2):
        y = lax.rem(m + MP - k, MP)
        bcopy(y, k, other).wait_recv()

    eye = iota((rows, rows), 0) == iota((rows, rows), 1)

    def to_col(row):
        return jnp.sum(jnp.where(eye, jnp.broadcast_to(row, (rows, rows)), 0.0), axis=1, keepdims=True)

    def to_row(col):
        return jnp.sum(jnp.where(eye, jnp.broadcast_to(col, (rows, rows)), 0.0), axis=0, keepdims=True)

    pick = (jnp.broadcast_to(to_col(pos), (rows, slots)) == iota((rows, slots), 1).astype(f32)).astype(bf16)
    acc = jnp.zeros((rows, cols), f32)
    for y in range(MP):
        a = jnp.dot(pick, ag[y].reshape(slots, ag.shape[-1]), preferred_element_type=f32).astype(bf16)
        acc = acc + jnp.dot(a, wc[y], preferred_element_type=f32)

    mean = jnp.sum(acc, axis=1, keepdims=True) / cols
    dev = acc - mean
    m2 = jnp.sum(dev * dev, axis=1, keepdims=True)
    st[0:1, :] = to_row(mean)
    st[1:2, :] = to_row(m2)

    def scopy(k, to):
        return pltpu.make_async_remote_copy(
            src_ref=st, dst_ref=sr.at[k], send_sem=sss.at[k], recv_sem=srs.at[k],
            device_id={"mp": to}, device_id_type=MESH)

    for k in (1, 3, 2):
        scopy(k, lax.rem(m + k, MP)).start()

    @pl.loop(1, NS)
    def _(k):
        d = seq_at(k)
        tcopy(d, s).wait_send()
        rcopy(d, s).wait_send()

    @pl.loop(0, NS)
    def _(c):
        drain1(c)
        drain2(c)

    for k in (1, 3, 2):
        wcopy(lax.rem(m + k, MP), k).wait_send()
        bcopy(lax.rem(m + MP - k, MP), k, mine).wait_send()

    for k in (1, 3, 2):
        scopy(k, lax.rem(m + k, MP)).wait()

    means = [st[0:1, :]] + [sr[k, 0:1, :] for k in (1, 2, 3)]
    m2s = [st[1:2, :]] + [sr[k, 1:2, :] for k in (1, 2, 3)]
    avg = sum(means) / MP
    sq = sum(m2s) + cols * sum((u - avg) * (u - avg) for u in means)
    rstd = lax.rsqrt(sq / (MP * cols) + EPS)
    avg_c = to_col(avg)
    rstd_c = to_col(rstd)
    own = pl.ds(pl.multiple_of(m * cols, 128), cols)
    n = (acc - avg_c) * rstd_c * qg_ref[:, own] + qb_ref[:, own]
    o_ref[...] = (x_ref[...].astype(f32) + n).astype(bf16)


def shards(
    patches, image_of, prompt_of, text_len, text_kv, w_qkv, w_out, pre_gain, pre_bias, post_gain, post_bias,
):
    NS = lax.axis_size("seq")
    MP = lax.axis_size("mp")
    rows, cols = patches.shape
    depth = rows // NS
    hc = w_out.shape[0]
    toks = text_kv.shape[1]
    text = jnp.transpose(text_kv, (0, 2, 1, 3))
    w = jnp.transpose(w_qkv, (1, 0, 2))
    full = w_qkv.shape[0]
    vm = pl.BlockSpec(memory_space=pltpu.VMEM)
    sm = pl.BlockSpec(memory_space=pltpu.SMEM)
    anys = pl.BlockSpec(memory_space=pl.ANY)
    dma = pltpu.SemaphoreType.DMA
    return pl.pallas_call(
        fused,
        out_shape=jax.ShapeDtypeStruct((rows, cols), bf16),
        in_specs=[vm, vm, sm, sm, vm, anys, anys, vm, vm, vm, vm],
        out_specs=vm,
        scratch_shapes=[
            pltpu.VMEM((NS, 2, depth, cols), bf16),
            pltpu.VMEM((MP, NS, 2, depth, cols), bf16),
            pltpu.VMEM((2, NS, depth, full), bf16),
            pltpu.VMEM((3, full, hc), bf16),
            pltpu.VMEM((MP, hc, cols), bf16),
            pltpu.VMEM((3, 2, NS * depth, hc), bf16),
            pltpu.VMEM((NS, 2, 2, toks, hc), bf16),
            pltpu.VMEM((NS, 2, 2, toks, hc), bf16),
            pltpu.VMEM((NS, 2, depth, hc), bf16),
            pltpu.VMEM((MP, NS, 2, depth, hc), bf16),
            pltpu.VMEM((1, 128), i32),
            pltpu.VMEM((NS, 1, 128), i32),
            pltpu.SMEM((NS, 1, 128), i32),
            pltpu.VMEM((8, rows), f32),
            pltpu.VMEM((MP, 8, rows), f32),
            pltpu.VMEM((4, 1, NS * depth), f32),
            dma((NS,)), dma((NS,)), dma((NS,)), dma((NS,)), dma((NS,)), dma((NS,)),
            dma((4, NS)), dma((4, NS)), dma((NS,)), dma((NS,)), dma((4, NS)), dma((4, NS)),
            dma((4,)), dma((4,)), dma((4,)), dma((4,)), dma((4,)), dma((4,)), dma((3,)),
        ],
        compiler_params=pltpu.CompilerParams(collective_id=0, has_side_effects=True, vmem_limit_bytes=50 << 20),
    )(
        patches, image_of.reshape(1, rows), prompt_of, text_len, text, w, w_out,
        pre_gain.reshape(1, -1), pre_bias.reshape(1, -1), post_gain.reshape(1, -1), post_bias.reshape(1, -1),
    )


def solution(mesh):
    placed = (
        P(("dp", "seq"), "mp"),
        P(("dp", "seq")),
        P("dp", "seq"),
        P("dp", None),
        P("dp", "seq", None, "mp"),
        P(None, None, "mp"),
        P("mp", None),
        P(),
        P(),
        P(),
        P(),
    )
    return jax.shard_map(
        shards, mesh=mesh, in_specs=placed, out_specs=P(("dp", "seq"), "mp"), check_vma=False
    )
```

time: 274 us -> 101 us (0.37); the launches traced: 270 us -> 101 us
  waiting for transfers between devices: 137 us -> 0 us
  Pallas kernels: 0 us -> 91.4 us
  blocking collectives: 39.7 us -> 0 us
  local copies, waits for them, and re-layouts: 35.6 us -> 9.26 us
  matrix products: 17.1 us -> 0 us
  other arithmetic: 15.7 us -> 0 us
  between operations: 13.5 us -> 0.03 us
  starting transfers between devices: 10.9 us -> 0 us
    pallas_call x0 -> x1, Pallas kernels: none -> 91.4 us  [shards(): pl.pallas_call(fused, out_shape=jax.ShapeDtypeStruct((rows, cols), bf16),...]
    reduce_scatter x1 -> x0, waiting for transfers between devices: 63.7 us -> none  [finish(): lax.psum_scatter(partial_sum, 'mp', scatter_dimension=1, tiled=True)]
    all_gather x2 -> x0, waiting for transfers between devices: 53 us -> none  [the longest x1 30.1 us: shards(): text_all = lax.all_gather(text_kv, 'seq', axis=1, tiled=True)]
    all_to_all x1 -> x0, blocking collectives: 30.9 us -> none  [dispatch(): lax.all_to_all(buffer, 'seq', split_axis=1, concat_axis=1, tiled=True)]
    all_to_all x2 -> x0, waiting for transfers between devices: 20.7 us -> none  [the longest x1 20.7 us: collect(): lax.all_to_all(slot_data, 'seq', split_axis=1, concat_axis=1, tiled=True)]
    dot_general x5 -> x0, matrix products: 17.1 us -> none  [the longest x1 7.7 us: project(): jnp.dot(normed, merged, preferred_element_type=jnp.float32)]
    all_to_all x2 -> x0, starting transfers between devices: 10.6 us -> none  [the longest x1 7.16 us: collect(): lax.all_to_all(slot_data, 'seq', split_axis=1, concat_axis=1, tiled=True)]
    psum x1 -> x0, blocking collectives: 8.79 us -> none  [finish(): lax.psum((jnp.sum(owned_part, axis=1), jnp.sum(owned_part * owned_part, a...]
  transfers between devices with their start and end apart: 5 -> 0, of which waited for: 4 -> 0; matrix products, arithmetic and copies ran while one was open for 12% -> 0% of each run, Pallas kernels for 0% -> 0%
where the time goes in v1:
time: 101 us
  Pallas kernels  91.4 us (90%)
  local copies, waits for them, and re-layouts  9.26 us (9%)
    pallas_call x1, Pallas kernels, shards(): pl.pallas_call(fused, out_shape=jax.ShapeDtypeStruct((rows, cols), bf16),...  91.4 us
    unnamed x20, local copies, waits for them, and re-layouts  9.26 us

profile of v1, /device:TPU:2, one launch (start us, length us, event | category | flops | bytes accessed | tf_op | source)
XLA Modules:
  0.0 100.7 jit_solution(6630615152831989213)
XLA Ops:
  0.0 1.0 %copy.14 = bf16[16,16,2,384]{3,1,2,0:T(8,128)(2,1)S(1)} copy(bf16[16,16,2,384]{3,2,1,0:T(2,128)(2,1)} %param.15) | data formatting | bytes 786432 | tf_op args[4]
  1.0 0.0 copy-start
  1.1 1.7 %copy-done = bf16[384,3072]{1,0:T(8,128)(2,1)S(1)} copy-done((bf16[384,3072]{1,0:T(8,128)(2,1)S(1)}, bf16[384,3072]{1,0:T(8,128)(2,1)}, u32[]{:S(2)}) %copy-start) | copy-done | bytes 2359320
  2.7 0.0 copy-start.1
  2.7 1.0 copy-done.1
  3.7 0.0 copy-start.2
  3.7 0.7 copy-done.2
  4.4 0.0 copy-start.3
  4.4 0.7 copy-done.3
  5.1 0.0 copy-start.4
  5.1 0.7 copy-done.4
  5.8 0.0 copy-start.5
  5.8 0.7 copy-done.5
  6.5 0.0 copy-start.6
  6.5 0.7 copy-done.6
  7.2 0.0 copy-start.7
  7.2 0.7 copy-done.7
  7.9 0.0 copy-start.8
  7.9 0.7 copy-done.8
  8.5 91.4 %shard_map.109 = bf16[256,768]{1,0:T(8,128)(2,1)S(1)} custom-call(bf16[256,768]{1,0:T(8,128)(2,1)S(1)} %copy-done.1, s32[1,256]{1,0:T(1,128)S(1)} %bitcast.14, s32[1,2]{1,0:T(1,128)S(1)} %copy-done.7, s32[1,16]{1,0:T(1,128)S(1)} %copy-done.8, bf16[16,2,16,384]{3,2,1,0:T(8,128)(2,1)S(1)} %bitcast.9, bf16[3,3072,384]{2,1,0:T(8,128)(2,1)} %bitcast.15, ...), custom_call_target="tpu_custom_call" | custom-call | tf_op jit(solution)/shard_map/pallas_call | solution.py:399
  100.0 0.7 copy.16
Async XLA Ops:
  1.0 1.7 %copy-start = (bf16[384,3072]{1,0:T(8,128)(2,1)S(1)}, bf16[384,3072]{1,0:T(8,128)(2,1)}, u32[]{:S(2)}) copy-start(bf16[384,3072]{1,0:T(8,128)(2,1)} %wo_ref.1) | copy-start | bytes 7077892
  2.7 1.0 copy-start.1
  3.7 0.7 copy-start.2
  4.4 0.7 copy-start.3
  5.1 0.7 copy-start.4
  5.8 0.7 copy-start.5
  6.5 0.7 copy-start.6
  7.2 0.7 copy-start.7
  7.9 0.7 copy-start.8

commit v2 on v1

--- a/solution.py
+++ b/solution.py
@@ -22,9 +22,9 @@
 
 
 def fused(
-    x_ref, img_ref, prm_ref, len_ref, text_ref, w_ref, wo_ref, pg_ref, pb_ref, qg_ref, qb_ref,
+    x_in, img_in, prm_ref, len_ref, text_ref, w_ref, wo_ref, pg_in, pb_in, qg_in, qb_in,
     o_ref,
-    xs, xg, xn, wv, wc, qkv, ts, tr, ret, ag, ms, mr, mrs, st, sr, kb,
+    x_ref, img_ref, pg_ref, pb_ref, qg_ref, qb_ref, xs, xg, xn, wv, wc, qkv, ts, tr, ret, ag, ms, mr, mrs, st, sr, kb,
     zss, zrs, tss, trs, mss, mrsem, yss, yrs, rss, rrs, y2s, y2r, wss, wrs, bss, brs, sss, srs, lsem,
 ):
     s = lax.axis_index("seq")
@@ -58,11 +58,18 @@
     for d in (right, left, far):
         pl.semaphore_signal(bar, inc=1, device_id={"mp": d}, device_id_type=MESH)
 
+    loads = []
+    for n, (a, b) in enumerate(
+        ((img_in, img_ref), (x_in, x_ref), (pg_in, pg_ref), (pb_in, pb_ref), (qg_in, qg_ref), (qb_in, qb_ref))
+    ):
+        loads.append(pltpu.make_async_copy(a, b, lsem.at[3 + n]))
+        loads[-1].start()
     wcp = pltpu.make_async_copy(w_ref, wv, lsem.at[0])
     wcp.start()
     ocp = pltpu.make_async_copy(wo_ref.at[:, pl.ds(pl.multiple_of(m * cols, 128), cols)], wc.at[m], lsem.at[1])
     ocp.start()
 
+    loads[0].wait()
     img = img_ref[...]
     onehot = (jnp.broadcast_to(img, (nimg, rows)) == iota((nimg, rows), 0)).astype(f32)
     upto = (iota((rows, rows), 0) <= iota((rows, rows), 1)).astype(bf16)
@@ -79,20 +86,21 @@
     ms[...] = crow
     mr[s] = crow
     place = (jnp.broadcast_to(pos, (slots, rows)) == iota((slots, rows), 0).astype(f32)).astype(bf16)
+    loads[1].wait()
     spread = jnp.dot(place, x_ref[...], preferred_element_type=f32).astype(bf16)
     xs[...] = spread.reshape(xs.shape)
     xg[m, s] = xs[s]
 
-    pl.semaphore_wait(bar, NS - 1 + 3)
+    pl.semaphore_wait(bar, NS - 1 + MP - 1)
 
     def zcopy(d, c):
         return pltpu.make_async_remote_copy(
             src_ref=xs.at[d], dst_ref=xg.at[m, c], send_sem=zss.at[d], recv_sem=zrs.at[c],
             device_id={"seq": d}, device_id_type=MESH)
 
-    def tcopy(d, c):
-        return pltpu.make_async_remote_copy(
-            src_ref=ts.at[d], dst_ref=tr.at[c], send_sem=tss.at[d], recv_sem=trs.at[c],
+    def tcopy(i, d, c):
+        return pltpu.make_async_remote_copy(
+            src_ref=ts.at[i, d], dst_ref=tr.at[i, c], send_sem=tss.at[i, d], recv_sem=trs.at[i, c],
             device_id={"seq": d}, device_id_type=MESH)
 
     def mcopy(d, c):
@@ -100,9 +108,9 @@
             src_ref=ms, dst_ref=mr.at[c], send_sem=mss.at[d], recv_sem=mrsem.at[c],
             device_id={"seq": d}, device_id_type=MESH)
 
-    def rcopy(d, c):
-        return pltpu.make_async_remote_copy(
-            src_ref=ret.at[d], dst_ref=ag.at[m, c], send_sem=rss.at[d], recv_sem=rrs.at[c],
+    def rcopy(i, d, c):
+        return pltpu.make_async_remote_copy(
+            src_ref=ret.at[i, d], dst_ref=ag.at[m, i, c], send_sem=rss.at[i, d], recv_sem=rrs.at[i, c],
             device_id={"seq": d}, device_id_type=MESH)
 
     def relay(buf, ssem, rsem):
@@ -141,32 +149,78 @@
 
         return open_, pass_on, arrived, drain
 
+    hrows = wc.shape[1] // 2
+
+    def half(co):
+        return pl.ds(pl.multiple_of(co * hrows, 16), hrows)
+
+    def wcopy(to, y, k):
+        return pltpu.make_async_remote_copy(
+            src_ref=wo_ref.at[half(core), pl.ds(pl.multiple_of(to * cols, 128), cols)], dst_ref=wc.at[y, half(core)],
+            send_sem=wss.at[k], recv_sem=wrs.at[k], device_id={"mp": to}, device_id_type=MESH)
+
+    def bcopy(y, k, part):
+        return pltpu.make_async_remote_copy(
+            src_ref=wc.at[y, part], dst_ref=wc.at[y, part], send_sem=bss.at[k], recv_sem=brs.at[k],
+            device_id={"seq": sib}, device_id_type=MESH)
+
+    YS = [(k, lax.rem(m + k, MP), lax.rem(m + MP - k, MP)) for k in (1, 3, 2)]
+
+    def wout_out():
+        for k, to, _ in YS:
+            wcopy(to, m, k).start()
+
+    def wout_over_cores():
+        for k, _, y in YS:
+            wcopy(y, y, k).wait_recv()
+            bcopy(y, k, half(core)).start()
+
+    def wout_in():
+        ocp.wait()
+        for k, _, y in YS:
+            bcopy(y, k, half(1 - core)).wait_recv()
+
+    def wout_drain():
+        for k, to, y in YS:
+            wcopy(to, m, k).wait_send()
+            bcopy(y, k, half(core)).wait_send()
+
     @pl.loop(1, NS)
     def _(k):
         mcopy(seq_at(k), s).start()
 
-    @pl.loop(1, NS)
+    AHEAD = 6
+
+    @pl.loop(1, 1 + AHEAD)
     def _(t):
         zcopy(seq_at(step_k(t)), s).start()
 
-    @pl.loop(1, NS)
-    def _(k):
-        c = seq_at(k)
-        mcopy(c, c).wait()
-
-    scp = pltpu.make_async_copy(mr, mrs, lsem.at[2])
-    scp.start()
-    scp.wait()
-
-    @pl.loop(0, NS)
-    def _(d):
+    open1, pass1, arrived1, drain1 = relay(xg, yss, yrs)
+    LAG1 = 6
+    LAG2 = 12
+    T0 = 10
+    TM = 4
+
+    def text_out():
+        @pl.loop(1, NS)
+        def _(k):
+            c = seq_at(k)
+            mcopy(c, c).wait()
+
+        scp = pltpu.make_async_copy(mr, mrs, lsem.at[2])
+        scp.start()
+        scp.wait()
+
+        @pl.loop(0, NS)
+        def _(d):
+            for i in range(2):
+                ts[i, d] = text_ref[mrs[d, 0, nimg + i]]
+
         for i in range(2):
-            ts[d, i] = text_ref[mrs[d, 0, nimg + i]]
-
-    tr[s] = ts[s]
-
-    open1, pass1, arrived1, drain1 = relay(xg, yss, yrs)
-    LAG1, LAG2 = 2, 4
+            tr[i, s] = ts[i, s]
+
+        for n in range(2, 6):
+            loads[n].wait()
 
     def norm_chunk(c):
         parts = [xg[y, c].astype(f32) for y in range(MP)]
@@ -199,7 +253,32 @@
             @pl.when(t > 0)
             def _():
                 zcopy(d, s).wait_send()
-                tcopy(d, s).start()
+
+            @pl.when((t > 0) & (t + AHEAD < NS))
+            def _():
+                zcopy(seq_at(step_k(t + AHEAD)), s).start()
+
+        @pl.when((t >= T0) & (t < T0 + 8))
+        def _():
+            for n in range(2):
+                j = 2 * (t - T0) + n
+
+                @pl.when(j > 0)
+                def _():
+                    tcopy(0, seq_at(step_k(j)), s).start()
+
+        @pl.when((t >= T0 + 8) & (t < T0 + 12))
+        def _():
+            for n in range(4):
+                j = 4 * (t - T0 - 8) + n
+
+                @pl.when(j > 0)
+                def _():
+                    tcopy(1, seq_at(step_k(j)), s).start()
+
+        @pl.when(t == TM)
+        def _():
+            text_out()
 
         @pl.when((t >= LAG1) & (t < NS + LAG1))
         def _():
@@ -211,28 +290,9 @@
             arrived1(c)
             norm_chunk(c)
 
-    hrows = wc.shape[1] // 2
-    mine = pl.ds(pl.multiple_of(core * hrows, 16), hrows)
-
-    def wcopy(y, k):
-        return pltpu.make_async_remote_copy(
-            src_ref=wo_ref.at[mine, pl.ds(pl.multiple_of(y * cols, 128), cols)], dst_ref=wc.at[m, mine],
-            send_sem=wss.at[k], recv_sem=wrs.at[k], device_id={"mp": y}, device_id_type=MESH)
-
-    def wgot(y, k):
-        return pltpu.make_async_remote_copy(
-            src_ref=wo_ref.at[mine, pl.ds(pl.multiple_of(y * cols, 128), cols)], dst_ref=wc.at[y, mine],
-            send_sem=wss.at[k], recv_sem=wrs.at[k], device_id={"mp": y}, device_id_type=MESH)
-
-    other = pl.ds(pl.multiple_of((1 - core) * hrows, 16), hrows)
-
-    def bcopy(y, k, part):
-        return pltpu.make_async_remote_copy(
-            src_ref=wc.at[y, part], dst_ref=wc.at[y, part], send_sem=bss.at[k], recv_sem=brs.at[k],
-            device_id={"seq": sib}, device_id_type=MESH)
-
-    for k in (1, 3, 2):
-        wcopy(lax.rem(m + k, MP), k).start()
+        @pl.when(t == NS + LAG1)
+        def _():
+            wout_out()
 
     wcp.wait()
     normed = xn[...].reshape(slots, MP * cols)
@@ -253,16 +313,16 @@
         n = len_ref[0, mrs[s, 0, nimg + i]]
         kb[2 * i + 1] = jnp.where(lanes < n, 0.0, NEG)
 
-    @pl.loop(1, NS)
-    def _(k):
-        c = seq_at(k)
-        tcopy(c, c).wait_recv()
-
     scale = 1.0 / math.sqrt(HD)
     nt = (((1,), (1,)), ((), ()))
 
     @pl.loop(0, 2)
     def _(i):
+        @pl.loop(1, NS)
+        def _(k):
+            c = seq_at(k)
+            tcopy(i, c, c).wait_recv()
+
         bi = kb[2 * i]
         bt = kb[2 * i + 1]
         for h in range(heads):
@@ -270,8 +330,8 @@
             q = qkv[0, i, :, hs]
             ki = qkv[1, i, :, hs]
             vi = qkv[2, i, :, hs]
-            kt = tr[:, i, 0, :, hs].reshape(tlen, HD)
-            vt = tr[:, i, 1, :, hs].reshape(tlen, HD)
+            kt = tr[i, :, 0, :, hs].reshape(tlen, HD)
+            vt = tr[i, :, 1, :, hs].reshape(tlen, HD)
             s1 = lax.dot_general(q, ki, nt, preferred_element_type=f32) * scale + bi
             s2 = lax.dot_general(q, kt, nt, preferred_element_type=f32) * scale + bt
             top = jnp.maximum(jnp.max(s1, axis=-1, keepdims=True), jnp.max(s2, axis=-1, keepdims=True))
@@ -282,45 +342,60 @@
             p1 = (e1 * inv).astype(bf16)
             p2 = (e2 * inv).astype(bf16)
             o = jnp.dot(p1, vi, preferred_element_type=f32) + jnp.dot(p2, vt, preferred_element_type=f32)
-            ret[:, i, :, hs] = o.astype(bf16).reshape(NS, depth, HD)
-
-    @pl.loop(1, NS)
-    def _(t):
-        rcopy(seq_at(step_k(t)), s).start()
-
-    ag[m, s] = ret[s]
-    for k in (1, 3, 2):
-        y = lax.rem(m + MP - k, MP)
-        wgot(y, k).wait_recv()
-        bcopy(y, k, mine).start()
-
-    open2, pass2, arrived2, drain2 = relay(ag, y2s, y2r)
-
-    @pl.loop(0, NS + LAG1)
-    def _(t):
-        @pl.when(t < NS)
-        def _():
-            k = step_k(t)
-            c = lax.rem(s + NS - k, NS)
-
-            @pl.when(t > 0)
-            def _():
-                rcopy(c, c).wait_recv()
-
-            open2(c)
-
-        @pl.when(t >= LAG1)
-        def _():
-            pass2(lax.rem(s + NS - step_k(t - LAG1), NS))
-
-    @pl.loop(0, NS)
-    def _(c):
-        arrived2(c)
-
-    ocp.wait()
-    for k in (1, 3, 2):
-        y = lax.rem(m + MP - k, MP)
-        bcopy(y, k, other).wait_recv()
+            ret[i, :, :, hs] = o.astype(bf16).reshape(NS, depth, HD)
+
+        ag[m, i, s] = ret[i, s]
+
+        @pl.loop(1, NS)
+        def _(t):
+            rcopy(i, seq_at(step_k(t)), s).start()
+
+    wout_over_cores()
+    GS = 4
+    NG = NS // GS
+    LAG3 = 3
+
+    def pass_two(i, g, src, to, n):
+        ref = ag.at[src, i, pl.ds(g * GS, GS)]
+        return pltpu.make_async_remote_copy(
+            src_ref=ref, dst_ref=ref, send_sem=y2s.at[n, i, g], recv_sem=y2r.at[n, i, g],
+            device_id={"mp": to}, device_id_type=MESH)
+
+    def unit(u):
+        i = u // NG
+        v = lax.rem(u, NG)
+        g = lax.rem(s // GS + jnp.where(v == 2, 3, jnp.where(v == 3, 2, v)), NG)
+        odd = lax.rem(g + i, 2)
+        return i, g, odd
+
+    @pl.loop(0, 2 * NG + LAG3)
+    def _(u):
+        @pl.when(u < 2 * NG)
+        def _():
+            i, g, _ = unit(u)
+            for n in range(GS):
+                c = g * GS + n
+
+                @pl.when(c != s)
+                def _():
+                    rcopy(i, c, c).wait_recv()
+
+            pass_two(i, g, m, right, 0).start()
+            pass_two(i, g, m, left, 1).start()
+
+        @pl.when(u >= LAG3)
+        def _():
+            i, g, odd = unit(u - LAG3)
+            pass_two(i, g, jnp.where(odd == 0, left, right), right, odd).wait_recv()
+            pass_two(i, g, jnp.where(odd == 0, left, right), jnp.where(odd == 0, right, left), 2).start()
+
+    wout_in()
+
+    @pl.loop(0, 2 * NG)
+    def _(u):
+        i, g, odd = unit(u)
+        pass_two(i, g, jnp.where(odd == 0, right, left), right, 1 - odd).wait_recv()
+        pass_two(i, g, far, right, 2).wait_recv()
 
     eye = iota((rows, rows), 0) == iota((rows, rows), 1)
 
@@ -330,7 +405,10 @@
     def to_row(col):
         return jnp.sum(jnp.where(eye, jnp.broadcast_to(col, (rows, rows)), 0.0), axis=0, keepdims=True)
 
-    pick = (jnp.broadcast_to(to_col(pos), (rows, slots)) == iota((rows, slots), 1).astype(f32)).astype(bf16)
+    img_f = img.astype(f32)
+    pair = jnp.floor(img_f * 0.5)
+    pos2 = (img_f - 2.0 * pair) * (NS * depth) + pair * depth + rank
+    pick = (jnp.broadcast_to(to_col(pos2), (rows, slots)) == iota((rows, slots), 1).astype(f32)).astype(bf16)
     acc = jnp.zeros((rows, cols), f32)
     for y in range(MP):
         a = jnp.dot(pick, ag[y].reshape(slots, ag.shape[-1]), preferred_element_type=f32).astype(bf16)
@@ -353,17 +431,21 @@
     @pl.loop(1, NS)
     def _(k):
         d = seq_at(k)
-        tcopy(d, s).wait_send()
-        rcopy(d, s).wait_send()
+        for i in range(2):
+            tcopy(i, d, s).wait_send()
+            rcopy(i, d, s).wait_send()
 
     @pl.loop(0, NS)
     def _(c):
         drain1(c)
-        drain2(c)
-
-    for k in (1, 3, 2):
-        wcopy(lax.rem(m + k, MP), k).wait_send()
-        bcopy(lax.rem(m + MP - k, MP), k, mine).wait_send()
+
+    @pl.loop(0, NG)
+    def _(g):
+        for i in range(2):
+            for n in range(3):
+                pass_two(i, g, m, right, n).wait_send()
+
+    wout_drain()
 
     for k in (1, 3, 2):
         scopy(k, lax.rem(m + k, MP)).wait()
@@ -399,30 +481,37 @@
     return pl.pallas_call(
         fused,
         out_shape=jax.ShapeDtypeStruct((rows, cols), bf16),
-        in_specs=[vm, vm, sm, sm, vm, anys, anys, vm, vm, vm, vm],
+        in_specs=[anys, anys, sm, sm, vm, anys, anys, anys, anys, anys, anys],
         out_specs=vm,
         scratch_shapes=[
+            pltpu.VMEM((rows, cols), bf16),
+            pltpu.VMEM((1, rows), i32),
+            pltpu.VMEM((1, full), f32),
+            pltpu.VMEM((1, full), f32),
+            pltpu.VMEM((1, full), f32),
+            pltpu.VMEM((1, full), f32),
             pltpu.VMEM((NS, 2, depth, cols), bf16),
             pltpu.VMEM((MP, NS, 2, depth, cols), bf16),
             pltpu.VMEM((2, NS, depth, full), bf16),
             pltpu.VMEM((3, full, hc), bf16),
             pltpu.VMEM((MP, hc, cols), bf16),
             pltpu.VMEM((3, 2, NS * depth, hc), bf16),
-            pltpu.VMEM((NS, 2, 2, toks, hc), bf16),
-            pltpu.VMEM((NS, 2, 2, toks, hc), bf16),
-            pltpu.VMEM((NS, 2, depth, hc), bf16),
-            pltpu.VMEM((MP, NS, 2, depth, hc), bf16),
+            pltpu.VMEM((2, NS, 2, toks, hc), bf16),
+            pltpu.VMEM((2, NS, 2, toks, hc), bf16),
+            pltpu.VMEM((2, NS, depth, hc), bf16),
+            pltpu.VMEM((MP, 2, NS, depth, hc), bf16),
             pltpu.VMEM((1, 128), i32),
             pltpu.VMEM((NS, 1, 128), i32),
             pltpu.SMEM((NS, 1, 128), i32),
             pltpu.VMEM((8, rows), f32),
             pltpu.VMEM((MP, 8, rows), f32),
             pltpu.VMEM((4, 1, NS * depth), f32),
-            dma((NS,)), dma((NS,)), dma((NS,)), dma((NS,)), dma((NS,)), dma((NS,)),
-            dma((4, NS)), dma((4, NS)), dma((NS,)), dma((NS,)), dma((4, NS)), dma((4, NS)),
-            dma((4,)), dma((4,)), dma((4,)), dma((4,)), dma((4,)), dma((4,)), dma((3,)),
+            dma((NS,)), dma((NS,)), dma((2, NS)), dma((2, NS)), dma((NS,)), dma((NS,)),
+            dma((4, NS)), dma((4, NS)), dma((2, NS)), dma((2, NS)), dma((3, 2, NS // 4)), dma((3, 2, NS // 4)),
+            dma((MP,)), dma((MP,)), dma((MP,)), dma((MP,)), dma((MP,)), dma((MP,)),
+            dma((9,)),
         ],
-        compiler_params=pltpu.CompilerParams(collective_id=0, has_side_effects=True, vmem_limit_bytes=50 << 20),
+        compiler_params=pltpu.CompilerParams(collective_id=0, has_side_effects=True, vmem_limit_bytes=58 << 20),
     )(
         patches, image_of.reshape(1, rows), prompt_of, text_len, text, w, w_out,
         pre_gain.reshape(1, -1), pre_bias.reshape(1, -1), post_gain.reshape(1, -1), post_bias.reshape(1, -1),

time: 101 us -> 82.7 us (0.82)
  Pallas kernels: 91.4 us -> 78.6 us
  local copies, waits for them, and re-layouts: 9.26 us -> 3.56 us
    pallas_call x1, Pallas kernels: 91.4 us -> 78.6 us  [shards(): pl.pallas_call(fused, out_shape=jax.ShapeDtypeStruct((rows, cols), bf16),...]
    unnamed x20 -> x2, local copies, waits for them, and re-layouts: 9.26 us -> 3.56 us
where the time goes in v2:
time: 82.7 us; the launch traced here: 82.2 us
  Pallas kernels  78.6 us (95%)
  local copies, waits for them, and re-layouts  3.56 us (4%)
    pallas_call x1, Pallas kernels, shards(): pl.pallas_call(fused, out_shape=jax.ShapeDtypeStruct((rows, cols), bf16),...  78.6 us
    unnamed x2, local copies, waits for them, and re-layouts  3.56 us

profile of v2, /device:TPU:2, one launch (start us, length us, event | category | flops | bytes accessed | tf_op | source)
XLA Modules:
  0.0 82.2 jit_solution(16223043763171636706)
XLA Ops:
  0.0 1.8 %copy.14 = bf16[16,16,2,384]{3,1,2,0:T(8,128)(2,1)} copy(bf16[16,16,2,384]{3,2,1,0:T(2,128)(2,1)} %param.15) | data formatting | bytes 786432 | tf_op args[4]
  1.8 78.6 %shard_map.109 = bf16[256,768]{1,0:T(8,128)(2,1)} custom-call(bf16[256,768]{1,0:T(8,128)(2,1)} %x_in.1, s32[1,256]{1,0:T(1,128)} %bitcast.15, s32[1,2]{1,0:T(1,128)} %prm_ref.1, s32[1,16]{1,0:T(1,128)} %len_ref.1, bf16[16,2,16,384]{3,2,1,0:T(8,128)(2,1)} %bitcast.10, bf16[3,3072,384]{2,1,0:T(8,128)(2,1)} %bitcast.9, bf16[384,3072]{1,0:T(8,128)(2,1)} %wo_ref.1, ...), custom_call_target="tpu_custom_call" | custom-call | tf_op jit(solution)/shard_map/pallas_call | solution.py:481
  80.4 1.8 %copy.16 = bf16[256,768]{1,0:T(8,128)(2,1)} copy(bf16[256,768]{1,0:T(8,128)(2,1)} %shard_map.109) | data formatting | bytes 786432

commit v3 on v2

v3 whole, which is shorter than its diff:
```python
import math

import jax
import jax.numpy as jnp
from jax import lax
from jax.experimental import pallas as pl
from jax.experimental.pallas import tpu as pltpu
from jax.sharding import PartitionSpec as P

HD = 128
EPS = 1e-05
MESH = pl.DeviceIdType.MESH
NEG = -1e30

f32 = jnp.float32
bf16 = jnp.bfloat16
i32 = jnp.int32


def iota(shape, dim):
    return lax.broadcasted_iota(i32, shape, dim)


def fused(
    x_in, img_in, prm_ref, len_ref, text_ref, w_ref, wo_ref, pg_in, pb_in, qg_in, qb_in,
    o_ref,
    x_ref, img_ref, pg_ref, pb_ref, qg_ref, qb_ref, xs, xg, xn, wv, wc, qkv, ts, tr, ret, rb, av, ms, mr, mrs, st, sr, kb,
    zss, zrs, tss, trs, mss, mrsem, yss, yrs, rss, rrs, y2s, y2r, wss, wrs, bss, brs, sss, srs, lsem,
):
    s = lax.axis_index("seq")
    m = lax.axis_index("mp")
    NS, MP = xg.shape[1], xg.shape[0]
    rows = x_ref.shape[0]
    cols = x_ref.shape[1]
    slots = xs.shape[2] * xs.shape[1] * NS
    depth = xs.shape[2]
    nimg = 2 * NS
    heads = qkv.shape[-1] // HD
    right = lax.rem(m + 1, MP)
    left = lax.rem(m + MP - 1, MP)
    far = lax.rem(m + 2, MP)
    core = lax.rem(s, 2)
    sib = s + 1 - 2 * core

    NP = NS // 2
    pair = s // 2

    def seq_at(k):
        return lax.rem(s + k, NS)

    def hop(v):
        far_by = (v + 1) // 2
        return jnp.where(lax.rem(v, 2) == 1, far_by, NP - far_by)

    def to_pair(v):
        return lax.rem(pair + hop(v), NP)

    def from_pair(v):
        return lax.rem(pair + 2 * NP - hop(v), NP)

    def source(r):
        return 2 * from_pair(r // 2) + lax.rem(r + core, 2)

    bar = pltpu.get_barrier_semaphore()

    @pl.loop(1, NS)
    def _(k):
        pl.semaphore_signal(bar, inc=1, device_id={"seq": seq_at(k)}, device_id_type=MESH)

    for d in (right, left, far):
        pl.semaphore_signal(bar, inc=1, device_id={"mp": d}, device_id_type=MESH)

    loads = []
    for n, (a, b) in enumerate(
        ((img_in, img_ref), (x_in, x_ref), (pg_in, pg_ref), (pb_in, pb_ref), (qg_in, qg_ref), (qb_in, qb_ref))
    ):
        loads.append(pltpu.make_async_copy(a, b, lsem.at[3 + n]))
        loads[-1].start()
    wcp = pltpu.make_async_copy(w_ref, wv, lsem.at[0])
    wcp.start()
    ocp = pltpu.make_async_copy(wo_ref.at[:, pl.ds(pl.multiple_of(m * cols, 128), cols)], wc.at[m], lsem.at[1])
    ocp.start()

    loads[0].wait()
    img = img_ref[...]
    onehot = (jnp.broadcast_to(img, (nimg, rows)) == iota((nimg, rows), 0)).astype(f32)
    upto = (iota((rows, rows), 0) <= iota((rows, rows), 1)).astype(bf16)
    cum = jnp.dot(onehot.astype(bf16), upto, preferred_element_type=f32)
    rank = jnp.sum(cum * onehot, axis=0, keepdims=True) - 1.0
    pos = img.astype(f32) * depth + rank
    counts = jnp.sum(onehot, axis=1, keepdims=True)
    crow = jnp.sum(
        jnp.where(iota((nimg, 128), 0) == iota((nimg, 128), 1), jnp.broadcast_to(counts, (nimg, 128)), 0.0),
        axis=0, keepdims=True,
    ).astype(i32)
    lane = iota((1, 128), 1)
    crow = jnp.where(lane == nimg, prm_ref[0, 0], jnp.where(lane == nimg + 1, prm_ref[0, 1], crow))
    ms[...] = crow
    mr[s] = crow
    place = (jnp.broadcast_to(pos, (slots, rows)) == iota((slots, rows), 0).astype(f32)).astype(bf16)
    loads[1].wait()
    spread = jnp.dot(place, x_ref[...], preferred_element_type=f32).astype(bf16)
    xs[...] = spread.reshape(xs.shape)
    xg[m, s] = xs[s]

    pl.semaphore_wait(bar, NS - 1 + MP - 1)

    def copy(src, dst, ss, rs, **to):
        return pltpu.make_async_remote_copy(
            src_ref=src, dst_ref=dst, send_sem=ss, recv_sem=rs, device_id=to, device_id_type=MESH)

    def zcopy(d):
        return copy(xs.at[d], xg.at[m, s], zss.at[0], zrs.at[s], seq=d)

    def zgot(c):
        copy(xg.at[m, c], xg.at[m, c], zss.at[0], zrs.at[c], seq=sib).wait_recv()

    def tcopy(i, d):
        return copy(ts.at[i, d], tr.at[i, s], tss.at[i], trs.at[i], seq=d)

    def mcopy(d):
        return copy(ms, mr.at[s], mss.at[0], mrsem.at[0], seq=d)

    def rcopy(h, r, d):
        return copy(ret.at[h, r], rb.at[h, s], rss.at[h], rrs.at[h], seq=d)

    def acopy(h, to):
        return copy(av.at[m, h], av.at[m, h], y2s.at[0], y2r.at[m], mp=to)

    most = pl.ds(0, NS - 1)

    def each_other(start):
        @pl.loop(1, NS)
        def _(r):
            start(2 * to_pair(r // 2) + lax.rem(r + core, 2)).start()

    def unit1(y, c, n, to):
        ref = xg.at[y, c] if n < 2 else xg.at[y, c, n - 2]
        return copy(ref, ref, yss.at[n], yrs.at[n, c], mp=to)

    def open1(j):
        unit1(m, j, 0, right).start()
        unit1(m, j, 1, left).start()

    def pass1(j):
        unit1(left, j, 0, right).wait_recv()
        unit1(left, j, 2, right).start()
        unit1(right, j, 1, left).wait_recv()
        unit1(right, j, 3, left).start()

    def arrived1(j):
        unit1(far, j, 2, right).wait_recv()
        unit1(far, j, 3, left).wait_recv()

    def drain1():
        for n in range(4):
            ref = xg.at[m] if n < 2 else xg.at[m, pl.ds(0, NP)]
            copy(ref, ref, yss.at[n], yrs.at[n, 0], mp=right).wait_send()

    hrows = wc.shape[1] // 2

    def half(co):
        return pl.ds(pl.multiple_of(co * hrows, 16), hrows)

    def wcopy(to, y, k):
        return pltpu.make_async_remote_copy(
            src_ref=wo_ref.at[half(core), pl.ds(pl.multiple_of(to * cols, 128), cols)], dst_ref=wc.at[y, half(core)],
            send_sem=wss.at[k], recv_sem=wrs.at[k], device_id={"mp": to}, device_id_type=MESH)

    def bcopy(y, k, part):
        return pltpu.make_async_remote_copy(
            src_ref=wc.at[y, part], dst_ref=wc.at[y, part], send_sem=bss.at[k], recv_sem=brs.at[k],
            device_id={"seq": sib}, device_id_type=MESH)

    YS = [(k, lax.rem(m + k, MP), lax.rem(m + MP - k, MP)) for k in (1, 3, 2)]

    def wout_out():
        for k, to, _ in YS:
            wcopy(to, m, k).start()

    def wout_over_cores():
        for k, _, y in YS:
            wcopy(y, y, k).wait_recv()
            bcopy(y, k, half(core)).start()

    def wout_in():
        ocp.wait()
        for k, _, y in YS:
            bcopy(y, k, half(1 - core)).wait_recv()

    def wout_drain():
        for k, to, y in YS:
            wcopy(to, m, k).wait_send()
            bcopy(y, k, half(core)).wait_send()

    each_other(mcopy)
    each_other(zcopy)

    LAG1 = 6
    LAG2 = 12
    TM = 4
    T0 = 8
    T1 = 14

    def text_out():
        copy(mr.at[most], mr.at[most], mss.at[0], mrsem.at[0], seq=sib).wait_recv()
        scp = pltpu.make_async_copy(mr, mrs, lsem.at[2])
        scp.start()
        scp.wait()

        @pl.loop(0, NS)
        def _(d):
            for i in range(2):
                ts[i, d] = text_ref[mrs[d, 0, nimg + i]]

        for i in range(2):
            tr[i, s] = ts[i, s]

        for n in range(2, 6):
            loads[n].wait()
        wcp.wait()

    def project(hf, j):
        r = jnp.dot(xn[hf].reshape(slots // 2, MP * cols), wv[j], preferred_element_type=f32).astype(bf16)
        qkv[j, :, hf] = r.reshape(2, slots // 4, r.shape[-1])

    def norm_chunk(c, hf, r):
        parts = [xg[y, c].astype(f32) for y in range(MP)]
        total = sum(jnp.sum(p, axis=-1, keepdims=True) for p in parts)
        mean = total / (MP * cols)
        parts = [p - mean for p in parts]
        var = sum(jnp.sum(p * p, axis=-1, keepdims=True) for p in parts) / (MP * cols)
        inv = lax.rsqrt(var + EPS)
        for y in range(MP):
            g = pg_ref[:, y * cols:(y + 1) * cols].reshape(1, 1, cols)
            b = pb_ref[:, y * cols:(y + 1) * cols].reshape(1, 1, cols)
            n = (parts[y] * inv * g + b).astype(bf16)
            for i in range(2):
                xn[hf, i, r, :, y * cols:(y + 1) * cols] = n[i]

    @pl.loop(0, NS + LAG2)
    def _(t):
        @pl.when((t > 0) & (t < NS))
        def _():
            zgot(source(t))

        @pl.when(t < NS)
        def _():
            open1(source(t))

        @pl.when(t == TM)
        def _():
            text_out()

        @pl.when(t == T0)
        def _():
            each_other(lambda d: tcopy(0, d))

        @pl.when(t == T1)
        def _():
            each_other(lambda d: tcopy(1, d))

        @pl.when((t >= LAG1) & (t < NS + LAG1))
        def _():
            pass1(source(t - LAG1))

        @pl.when(t == NS + LAG1)
        def _():
            wout_out()

        @pl.when(t >= LAG2)
        def _():
            c = source(t - LAG2)
            arrived1(c)
            norm_chunk(c, (t - LAG2) // NP, lax.rem(t - LAG2, NP))

        @pl.when((t >= LAG2 + NP - 1) & (t < LAG2 + NP + 2))
        def _():
            project(0, t - (LAG2 + NP - 1))

    @pl.loop(0, 3)
    def _(j):
        project(1, j)

    span = NS * depth
    lanes = iota((1, span), 1)
    tlen = NS * depth
    for i in range(2):
        cnt = jnp.zeros((1, span), i32)
        for r in range(NS):
            cnt = jnp.where(lanes // depth == r, mrs[source(r), 0, 2 * s + i], cnt)
        kb[2 * i] = jnp.where(lax.rem(lanes, depth) < cnt, 0.0, NEG)
        n = len_ref[0, mrs[s, 0, nimg + i]]
        kb[2 * i + 1] = jnp.where(lanes < n, 0.0, NEG)

    scale = 1.0 / math.sqrt(HD)
    nt = (((1,), (1,)), ((), ()))
    for i in range(2):
        copy(tr.at[i, most], tr.at[i, most], tss.at[i], trs.at[i], seq=sib).wait_recv()

    for h in range(heads):
        hs = slice(h * HD, (h + 1) * HD)

        @pl.loop(0, 2)
        def _(i):
            bi = kb[2 * i]
            bt = kb[2 * i + 1]
            q, ki, vi = (qkv[n, i, :, :, hs].reshape(tlen, HD) for n in range(3))
            kt = tr[i, :, 0, :, hs].reshape(tlen, HD)
            vt = tr[i, :, 1, :, hs].reshape(tlen, HD)
            s1 = lax.dot_general(q, ki, nt, preferred_element_type=f32) * scale + bi
            s2 = lax.dot_general(q, kt, nt, preferred_element_type=f32) * scale + bt
            top = jnp.maximum(jnp.max(s1, axis=-1, keepdims=True), jnp.max(s2, axis=-1, keepdims=True))
            e1 = jnp.exp(s1 - top)
            e2 = jnp.exp(s2 - top)
            tot = jnp.sum(e1, axis=-1, keepdims=True) + jnp.sum(e2, axis=-1, keepdims=True)
            inv = 1.0 / tot
            p1 = (e1 * inv).astype(bf16)
            p2 = (e2 * inv).astype(bf16)
            o = jnp.dot(p1, vi, preferred_element_type=f32) + jnp.dot(p2, vt, preferred_element_type=f32)
            ret[h, :, i] = o.astype(bf16).reshape(NS, depth, HD)

        rb[h, s] = ret[h, 0]

        @pl.loop(1, NS)
        def _(r):
            rcopy(h, r, source(r)).start()

    eye = iota((rows, rows), 0) == iota((rows, rows), 1)

    def to_col(row):
        return jnp.sum(jnp.where(eye, jnp.broadcast_to(row, (rows, rows)), 0.0), axis=1, keepdims=True)

    def to_row(col):
        return jnp.sum(jnp.where(eye, jnp.broadcast_to(col, (rows, rows)), 0.0), axis=0, keepdims=True)

    pick = (jnp.broadcast_to(to_col(pos), (rows, slots)) == iota((rows, slots), 1).astype(f32)).astype(bf16)
    wout_over_cores()
    for h in range(heads):
        copy(rb.at[h, most], rb.at[h, most], rss.at[h], rrs.at[h], seq=sib).wait_recv()
        av[m, h] = jnp.dot(pick, rb[h].reshape(slots, HD), preferred_element_type=f32).astype(bf16)
        for to in (right, left, far):
            acopy(h, to).start()

    wout_in()

    def part(y):
        a = jnp.concatenate([av[y, h] for h in range(heads)], axis=1)
        return jnp.dot(a, wc[y], preferred_element_type=f32)

    acc = part(m)
    for y in (right, left, far):
        copy(av.at[y], av.at[y], y2s.at[0], y2r.at[y], mp=right).wait_recv()
        acc = acc + part(y)

    mean = jnp.sum(acc, axis=1, keepdims=True) / cols
    dev = acc - mean
    m2 = jnp.sum(dev * dev, axis=1, keepdims=True)
    st[0:1, :] = to_row(mean)
    st[1:2, :] = to_row(m2)

    def scopy(k, to):
        return pltpu.make_async_remote_copy(
            src_ref=st, dst_ref=sr.at[k], send_sem=sss.at[k], recv_sem=srs.at[k],
            device_id={"mp": to}, device_id_type=MESH)

    for k in (1, 3, 2):
        scopy(k, lax.rem(m + k, MP)).start()

    copy(mr.at[most], mr.at[most], mss.at[0], mrsem.at[0], seq=sib).wait_send()
    copy(xs.at[most], xs.at[most], zss.at[0], zrs.at[0], seq=sib).wait_send()
    for i in range(2):
        copy(ts.at[i, most], ts.at[i, most], tss.at[i], trs.at[i], seq=sib).wait_send()
    for h in range(heads):
        copy(ret.at[h, most], ret.at[h, most], rss.at[h], rrs.at[h], seq=sib).wait_send()
    drain1()
    copy(av.at[pl.ds(0, MP - 1)], av.at[pl.ds(0, MP - 1)], y2s.at[0], y2r.at[0], mp=right).wait_send()
    wout_drain()

    for k in (1, 3, 2):
        scopy(k, lax.rem(m + k, MP)).wait()

    means = [st[0:1, :]] + [sr[k, 0:1, :] for k in (1, 2, 3)]
    m2s = [st[1:2, :]] + [sr[k, 1:2, :] for k in (1, 2, 3)]
    avg = sum(means) / MP
    sq = sum(m2s) + cols * sum((u - avg) * (u - avg) for u in means)
    rstd = lax.rsqrt(sq / (MP * cols) + EPS)
    avg_c = to_col(avg)
    rstd_c = to_col(rstd)
    own = pl.ds(pl.multiple_of(m * cols, 128), cols)
    n = (acc - avg_c) * rstd_c * qg_ref[:, own] + qb_ref[:, own]
    o_ref[...] = (x_ref[...].astype(f32) + n).astype(bf16)


def shards(
    patches, image_of, prompt_of, text_len, text_kv, w_qkv, w_out, pre_gain, pre_bias, post_gain, post_bias,
):
    NS = lax.axis_size("seq")
    MP = lax.axis_size("mp")
    rows, cols = patches.shape
    depth = rows // NS
    hc = w_out.shape[0]
    toks = text_kv.shape[1]
    heads = hc // HD
    text = jnp.transpose(text_kv, (0, 2, 1, 3))
    w = jnp.transpose(w_qkv, (1, 0, 2))
    full = w_qkv.shape[0]
    vm = pl.BlockSpec(memory_space=pltpu.VMEM)
    sm = pl.BlockSpec(memory_space=pltpu.SMEM)
    anys = pl.BlockSpec(memory_space=pl.ANY)
    dma = pltpu.SemaphoreType.DMA
    return pl.pallas_call(
        fused,
        out_shape=jax.ShapeDtypeStruct((rows, cols), bf16),
        in_specs=[anys, anys, sm, sm, vm, anys, anys, anys, anys, anys, anys],
        out_specs=vm,
        scratch_shapes=[
            pltpu.VMEM((rows, cols), bf16),
            pltpu.VMEM((1, rows), i32),
            pltpu.VMEM((1, full), f32),
            pltpu.VMEM((1, full), f32),
            pltpu.VMEM((1, full), f32),
            pltpu.VMEM((1, full), f32),
            pltpu.VMEM((NS, 2, depth, cols), bf16),
            pltpu.VMEM((MP, NS, 2, depth, cols), bf16),
            pltpu.VMEM((2, 2, NS // 2, depth, full), bf16),
            pltpu.VMEM((3, full, hc), bf16),
            pltpu.VMEM((MP, hc, cols), bf16),
            pltpu.VMEM((3, 2, 2, NS * depth // 2, hc), bf16),
            pltpu.VMEM((2, NS, 2, toks, hc), bf16),
            pltpu.VMEM((2, NS, 2, toks, hc), bf16),
            pltpu.VMEM((heads, NS, 2, depth, HD), bf16),
            pltpu.VMEM((heads, NS, 2, depth, HD), bf16),
            pltpu.VMEM((MP, heads, rows, HD), bf16),
            pltpu.VMEM((1, 128), i32),
            pltpu.VMEM((NS, 1, 128), i32),
            pltpu.SMEM((NS, 1, 128), i32),
            pltpu.VMEM((8, rows), f32),
            pltpu.VMEM((MP, 8, rows), f32),
            pltpu.VMEM((4, 1, NS * depth), f32),
            dma((1,)), dma((NS,)), dma((2,)), dma((2,)), dma((1,)), dma((1,)),
            dma((4,)), dma((4, NS)), dma((heads,)), dma((heads,)), dma((1,)), dma((MP,)),
            dma((MP,)), dma((MP,)), dma((MP,)), dma((MP,)), dma((MP,)), dma((MP,)),
            dma((9,)),
        ],
        compiler_params=pltpu.CompilerParams(collective_id=0, has_side_effects=True, vmem_limit_bytes=58 << 20),
    )(
        patches, image_of.reshape(1, rows), prompt_of, text_len, text, w, w_out,
        pre_gain.reshape(1, -1), pre_bias.reshape(1, -1), post_gain.reshape(1, -1), post_bias.reshape(1, -1),
    )


def solution(mesh):
    placed = (
        P(("dp", "seq"), "mp"),
        P(("dp", "seq")),
        P("dp", "seq"),
        P("dp", None),
        P("dp", "seq", None, "mp"),
        P(None, None, "mp"),
        P("mp", None),
        P(),
        P(),
        P(),
        P(),
    )
    return jax.shard_map(
        shards, mesh=mesh, in_specs=placed, out_specs=P(("dp", "seq"), "mp"), check_vma=False
    )
```

time: 82.7 us -> 76.5 us (0.925)
  Pallas kernels: 78.6 us -> 72.8 us
    pallas_call x1, Pallas kernels: 78.6 us -> 72.8 us  [shards(): pl.pallas_call(fused, out_shape=jax.ShapeDtypeStruct((rows, cols), bf16),...]
where the time goes in v3:
time: 76.5 us; the launch traced here: 76.3 us
  Pallas kernels  72.8 us (95%)
  local copies, waits for them, and re-layouts  3.56 us (5%)
    pallas_call x1, Pallas kernels, shards(): pl.pallas_call(fused, out_shape=jax.ShapeDtypeStruct((rows, cols), bf16),...  72.8 us
    unnamed x2, local copies, waits for them, and re-layouts  3.56 us

profile of v3, /device:TPU:2, one launch (start us, length us, event | category | flops | bytes accessed | tf_op | source)
XLA Modules:
  0.0 76.3 jit_solution(17427051868328401689)
XLA Ops:
  0.0 1.8 %copy.14 = bf16[16,16,2,384]{3,1,2,0:T(8,128)(2,1)} copy(bf16[16,16,2,384]{3,2,1,0:T(2,128)(2,1)} %param.15) | data formatting | bytes 786432 | tf_op args[4]
  1.8 72.8 %shard_map.109 = bf16[256,768]{1,0:T(8,128)(2,1)} custom-call(bf16[256,768]{1,0:T(8,128)(2,1)} %x_in.1, s32[1,256]{1,0:T(1,128)} %bitcast.15, s32[1,2]{1,0:T(1,128)} %prm_ref.1, s32[1,16]{1,0:T(1,128)} %len_ref.1, bf16[16,2,16,384]{3,2,1,0:T(8,128)(2,1)} %bitcast.10, bf16[3,3072,384]{2,1,0:T(8,128)(2,1)} %bitcast.9, bf16[384,3072]{1,0:T(8,128)(2,1)} %wo_ref.1, ...), custom_call_target="tpu_custom_call" | custom-call | tf_op jit(solution)/shard_map/pallas_call | solution.py:412
  74.6 1.8 %copy.16 = bf16[256,768]{1,0:T(8,128)(2,1)} copy(bf16[256,768]{1,0:T(8,128)(2,1)} %shard_map.109) | data formatting | bytes 786432

commit v4 on v3

--- a/solution.py
+++ b/solution.py
@@ -24,7 +24,7 @@
 def fused(
     x_in, img_in, prm_ref, len_ref, text_ref, w_ref, wo_ref, pg_in, pb_in, qg_in, qb_in,
     o_ref,
-    x_ref, img_ref, pg_ref, pb_ref, qg_ref, qb_ref, xs, xg, xn, wv, wc, qkv, ts, tr, ret, rb, av, ms, mr, mrs, st, sr, kb,
+    x_ref, img_ref, pg_ref, pb_ref, qg_ref, qb_ref, xs, xg, xn, wv, wc, qkv, ts, tr, ret, rb, av, tx, ms, mr, mrs, st, sr, kb,
     zss, zrs, tss, trs, mss, mrsem, yss, yrs, rss, rrs, y2s, y2r, wss, wrs, bss, brs, sss, srs, lsem,
 ):
     s = lax.axis_index("seq")
@@ -72,7 +72,7 @@
 
     loads = []
     for n, (a, b) in enumerate(
-        ((img_in, img_ref), (x_in, x_ref), (pg_in, pg_ref), (pb_in, pb_ref), (qg_in, qg_ref), (qb_in, qb_ref))
+        ((img_in, img_ref), (x_in, x_ref), (pg_in, pg_ref), (pb_in, pb_ref), (qg_in, qg_ref), (qb_in, qb_ref), (text_ref, tx))
     ):
         loads.append(pltpu.make_async_copy(a, b, lsem.at[3 + n]))
         loads[-1].start()
@@ -203,6 +203,7 @@
     T1 = 14
 
     def text_out():
+        loads[6].wait()
         copy(mr.at[most], mr.at[most], mss.at[0], mrsem.at[0], seq=sib).wait_recv()
         scp = pltpu.make_async_copy(mr, mrs, lsem.at[2])
         scp.start()
@@ -211,7 +212,9 @@
         @pl.loop(0, NS)
         def _(d):
             for i in range(2):
-                ts[i, d] = text_ref[mrs[d, 0, nimg + i]]
+                both = tx[mrs[d, 0, nimg + i]]
+                ts[i, d, 0] = both[:, 0, :]
+                ts[i, d, 1] = both[:, 1, :]
 
         for i in range(2):
             tr[i, s] = ts[i, s]
@@ -402,7 +405,7 @@
     hc = w_out.shape[0]
     toks = text_kv.shape[1]
     heads = hc // HD
-    text = jnp.transpose(text_kv, (0, 2, 1, 3))
+    text = text_kv
     w = jnp.transpose(w_qkv, (1, 0, 2))
     full = w_qkv.shape[0]
     vm = pl.BlockSpec(memory_space=pltpu.VMEM)
@@ -412,7 +415,7 @@
     return pl.pallas_call(
         fused,
         out_shape=jax.ShapeDtypeStruct((rows, cols), bf16),
-        in_specs=[anys, anys, sm, sm, vm, anys, anys, anys, anys, anys, anys],
+        in_specs=[anys, anys, sm, sm, anys, anys, anys, anys, anys, anys, anys],
         out_specs=vm,
         scratch_shapes=[
             pltpu.VMEM((rows, cols), bf16),
@@ -432,6 +435,7 @@
             pltpu.VMEM((heads, NS, 2, depth, HD), bf16),
             pltpu.VMEM((heads, NS, 2, depth, HD), bf16),
             pltpu.VMEM((MP, heads, rows, HD), bf16),
+            pltpu.VMEM(text_kv.shape, bf16),
             pltpu.VMEM((1, 128), i32),
             pltpu.VMEM((NS, 1, 128), i32),
             pltpu.SMEM((NS, 1, 128), i32),
@@ -441,7 +445,7 @@
             dma((1,)), dma((NS,)), dma((2,)), dma((2,)), dma((1,)), dma((1,)),
             dma((4,)), dma((4, NS)), dma((heads,)), dma((heads,)), dma((1,)), dma((MP,)),
             dma((MP,)), dma((MP,)), dma((MP,)), dma((MP,)), dma((MP,)), dma((MP,)),
-            dma((9,)),
+            dma((10,)),
         ],
         compiler_params=pltpu.CompilerParams(collective_id=0, has_side_effects=True, vmem_limit_bytes=58 << 20),
     )(

time: 76.5 us -> 74.3 us (0.971)
  local copies, waits for them, and re-layouts: 3.56 us -> 1.77 us
    unnamed x2 -> x1, local copies, waits for them, and re-layouts: 3.56 us -> 1.77 us
where the time goes in v4:
time: 74.3 us; the launch traced here: 74.2 us
  Pallas kernels  72.4 us (97%)
  local copies, waits for them, and re-layouts  1.77 us (2%)
    pallas_call x1, Pallas kernels, shards(): pl.pallas_call(fused, out_shape=jax.ShapeDtypeStruct((rows, cols), bf16),...  72.4 us
    unnamed x1, local copies, waits for them, and re-layouts  1.77 us

profile of v4, /device:TPU:2, one launch (start us, length us, event | category | flops | bytes accessed | tf_op | source)
XLA Modules:
  0.0 74.2 jit_solution(1657271344039542802)
XLA Ops:
  0.0 72.4 %shard_map.109 = bf16[256,768]{1,0:T(8,128)(2,1)} custom-call(bf16[256,768]{1,0:T(8,128)(2,1)} %x_in.1, s32[1,256]{1,0:T(1,128)} %bitcast.11, s32[1,2]{1,0:T(1,128)} %prm_ref.1, s32[1,16]{1,0:T(1,128)} %len_ref.1, bf16[16,16,2,384]{3,2,1,0:T(2,128)(2,1)} %text_ref.1, bf16[3,3072,384]{2,1,0:T(8,128)(2,1)} %bitcast.6, bf16[384,3072]{1,0:T(8,128)(2,1)} %wo_ref.1, ...), custom_call_target="tpu_custom_call" | custom-call | tf_op jit(solution)/shard_map/pallas_call | solution.py:415
  72.4 1.8 %copy.13 = bf16[256,768]{1,0:T(8,128)(2,1)} copy(bf16[256,768]{1,0:T(8,128)(2,1)} %shard_map.109) | data formatting | bytes 786432

commit v5 on v4

--- a/solution.py
+++ b/solution.py
@@ -193,12 +193,13 @@
             wcopy(to, m, k).wait_send()
             bcopy(y, k, half(core)).wait_send()
 
+    open1(s)
     each_other(mcopy)
     each_other(zcopy)
 
     LAG1 = 6
     LAG2 = 12
-    TM = 4
+    TM = 6
     T0 = 8
     T1 = 14
 
@@ -247,7 +248,7 @@
         def _():
             zgot(source(t))
 
-        @pl.when(t < NS)
+        @pl.when((t > 0) & (t < NS))
         def _():
             open1(source(t))
 

time: 74.3 us -> 74.3 us (level)
  no operation moved by 1% of the time
where the time goes in v5:
time: 74.3 us; the launch traced here: 74.2 us
  Pallas kernels  72.4 us (97%)
  local copies, waits for them, and re-layouts  1.77 us (2%)
    pallas_call x1, Pallas kernels, shards(): pl.pallas_call(fused, out_shape=jax.ShapeDtypeStruct((rows, cols), bf16),...  72.4 us
    unnamed x1, local copies, waits for them, and re-layouts  1.77 us

profile of v5, /device:TPU:2, one launch (start us, length us, event | category | flops | bytes accessed | tf_op | source)
XLA Modules:
  0.0 74.2 jit_solution(4835755994918163192)
XLA Ops:
  0.0 72.4 %shard_map.109 = bf16[256,768]{1,0:T(8,128)(2,1)} custom-call(bf16[256,768]{1,0:T(8,128)(2,1)} %x_in.1, s32[1,256]{1,0:T(1,128)} %bitcast.11, s32[1,2]{1,0:T(1,128)} %prm_ref.1, s32[1,16]{1,0:T(1,128)} %len_ref.1, bf16[16,16,2,384]{3,2,1,0:T(2,128)(2,1)} %text_ref.1, bf16[3,3072,384]{2,1,0:T(8,128)(2,1)} %bitcast.6, bf16[384,3072]{1,0:T(8,128)(2,1)} %wo_ref.1, ...), custom_call_target="tpu_custom_call" | custom-call | tf_op jit(solution)/shard_map/pallas_call | solution.py:416
  72.4 1.8 %copy.13 = bf16[256,768]{1,0:T(8,128)(2,1)} copy(bf16[256,768]{1,0:T(8,128)(2,1)} %shard_map.109) | data formatting | bytes 786432
